TPU v7x, 32 devices: a whole 2x2x4 slice. The times are simulated.
32 devices in a mesh: groups: 2 (over y), pool: 4 (over x, core), tp: 4 (over z).
Axes of the slice: x: 2, y: 2, z: 4, core: 2. Of those that a mesh axis runs over, the one named last changes fastest.
Arguments:
- queries: bfloat16 [4, 512, 8192], P('groups', 'pool', 'tp'), parts along dimension 0, may hold values from -4.5 to 4.5
- span_kv: bfloat16 [4, 512, 8, 256], P('groups', 'pool'), parts along dimension 0, may hold values from -4.5 to 4.5
- prefix_pool: bfloat16 [192, 128, 8, 256], P(('groups', 'pool'), 'tp'), parts along dimension 0, may hold values from -4.5 to 4.5
- hit_blocks: int32 [4, 24], P('groups'), parts along dimension 0, may hold values from 0 to 95, as said below
- prefix_len: int32 [4], P('groups'), parts along dimension 0, may hold values from 12 to 24, as said below
- dest_blocks: int32 [4, 4], P('groups'), parts along dimension 0, may hold values from 0 to 95, as said below
- out_w: bfloat16 [8192, 8192], P('tp'), may hold values from -0.375 to 0.375
- residual: bfloat16 [4, 512, 8192], P('groups', 'pool', 'tp'), parts along dimension 0, may hold values from -3 to 3
- norm_gain: bfloat16 [8192], P('tp'), may hold values from 0.5 to 1.5
Outputs:
- hidden: bfloat16 [4, 512, 8192], P('groups', 'pool', 'tp'), parts along dimension 0
- normed: bfloat16 [4, 512, 8192], P('groups', 'pool', 'tp'), parts along dimension 0
- new_pool: bfloat16 [192, 128, 8, 256], P(('groups', 'pool'), 'tp'), parts along dimension 0
There are 2 independent parts, one for each index of `groups`. A program takes and returns all parts, laid end to end along the dimension named above; an argument that names none is the same for every part. Nothing has to cross between parts.
Inputs may be any that keep to these rules, and one draw needn't show every extreme that they name: Block ids in hit_blocks are all distinct. Row j's first prefix_len[j] entries are prompt j's prefix blocks in order; later entries are unused. Block b lies on pool index b // 24. Over both prompts at most 12 used entries lie on one pool index, and some pool index holds exactly 12. `prefix_len`: one prompt has exactly 24 prefix blocks. `dest_blocks`: all distinct, and none appears in hit_blocks.
All inputs are finite; a program needn't handle non-finite values.
Results may differ from a plain program's by a relative error of at most 0.008.
Values may be sent and summed in bfloat16 or wider, within the bound.
No kernel may reach another device: no remote copies, remote signals or barrier semaphores. Data moves between devices by JAX's collectives and lax.ppermute only.
A program may use at most 192 MiB of HBM per device.

v0:
```python
import math

import jax
import jax.numpy as jnp
from jax import lax
from jax.sharding import PartitionSpec as P

QH = 64
KVH = 8
HD = 128
MAXB = 24
MOST = 12


floor_score = -1e30
epsilon = 1e-05


def online_update(running, scores, visible, values, pattern):
    maxima, totals, weighted = running
    scores = jnp.where(visible, scores, floor_score)
    new_max = jnp.maximum(maxima, jnp.max(scores, axis=-1))
    weights = jnp.where(visible, jnp.exp(scores - new_max[..., None]), 0.0)
    factor = jnp.exp(maxima - new_max)
    totals = totals * factor + jnp.sum(weights, axis=-1)
    weighted = weighted * factor[..., None] + jnp.einsum(
        pattern, weights, values.astype(jnp.float32)
    )
    return (new_max, totals, weighted)


def local(
    queries, span_kv, prefix_pool, hit_blocks, prefix_len, dest_blocks, out_w, residual, norm_gain
):
    tp_count = lax.axis_size("tp")
    tp_index = lax.axis_index("tp")
    pool_count = lax.axis_size("pool")
    pool_index = lax.axis_index("pool")
    prompts = queries.shape[0]
    rows_dev = queries.shape[1]
    heads_dev = queries.shape[2] // HD
    sharing = QH // KVH
    kv_dev = max(1, heads_dev // sharing)
    local_heads = heads_dev // kv_dev
    kv_first = tp_index * heads_dev // sharing
    block_rows = prefix_pool.shape[1]
    slots_dev = prefix_pool.shape[0]
    score_scale = 1.0 / math.sqrt(HD)
    query_grid = queries.reshape(prompts, rows_dev, kv_dev, local_heads, HD)
    query_pos = pool_index * rows_dev + jnp.arange(rows_dev)
    flat_ids = hit_blocks.reshape(-1)
    live_mask = (jnp.arange(MAXB)[None, :] < prefix_len[:, None]).reshape(-1)
    holder = flat_ids // slots_dev
    onehot = ((holder[:, None] == jnp.arange(pool_count)[None, :]) & live_mask[:, None]).astype(
        jnp.int32
    )
    slot_rank = jnp.sum((jnp.cumsum(onehot, axis=0) - 1) * onehot, axis=1)
    entry_slot = jnp.where(live_mask, holder * MOST + slot_rank, 0)
    matches = onehot[:, :, None] * (
        slot_rank[:, None, None] == jnp.arange(MOST)[None, None, :]
    ).astype(jnp.int32)
    slot_local = jnp.sum(matches * (flat_ids % slots_dev)[:, None, None], axis=0)
    own_slots = lax.dynamic_index_in_dim(slot_local, pool_index, 0, keepdims=False)
    held_blocks = jnp.take(prefix_pool, own_slots, axis=0)
    head_index = jnp.arange(tp_count)[:, None] * heads_dev // sharing + jnp.arange(kv_dev)[None, :]
    initial = (
        jnp.full((prompts, rows_dev, kv_dev, local_heads), floor_score, jnp.float32),
        jnp.zeros((prompts, rows_dev, kv_dev, local_heads), jnp.float32),
        jnp.zeros((prompts, rows_dev, kv_dev, local_heads, HD), jnp.float32),
    )
    span_heads = lax.dynamic_slice_in_dim(span_kv, kv_first, kv_dev, 2)
    span_portion = lax.all_gather(span_heads, "pool", axis=1, tiled=True)
    span_key_pos = jnp.arange(span_portion.shape[1])
    span_scores = (
        jnp.einsum(
            "pikgd,pnkd->pikgn",
            query_grid,
            span_portion[..., :HD],
            preferred_element_type=jnp.float32,
        )
        * score_scale
    )
    span_visible = (span_key_pos[None, :] <= query_pos[:, None])[None, :, None, None, :]
    running = online_update(
        initial, span_scores, span_visible, span_portion[..., HD:], "pikgn,pnkd->pikgd"
    )
    everyone = lax.all_gather(held_blocks, "pool", axis=0, tiled=True)
    outgoing = jnp.take(everyone, head_index, axis=2)
    arrived = lax.all_to_all(outgoing, "tp", split_axis=2, concat_axis=1, tiled=True)
    arrived = arrived.reshape(arrived.shape[0], arrived.shape[1], kv_dev, 2 * HD)
    prefix_running = running
    full_rows = arrived.shape[1]
    ordered = jnp.take(arrived, entry_slot, axis=0)
    ordered = ordered.reshape(prompts, MAXB, full_rows, kv_dev, 2 * HD)
    step_blocks = 8
    for start in range(0, MAXB, step_blocks):
        stop = min(MAXB, start + step_blocks)
        portion = ordered[:, start:stop].reshape(
            prompts, (stop - start) * full_rows, kv_dev, 2 * HD
        )
        key_pos = start * full_rows + jnp.arange((stop - start) * full_rows)
        scores = (
            jnp.einsum(
                "pikgd,pnkd->pikgn",
                query_grid,
                portion[..., :HD],
                preferred_element_type=jnp.float32,
            )
            * score_scale
        )
        visible = (key_pos[None, :] < prefix_len[:, None] * full_rows)[:, None, None, None, :]
        prefix_running = online_update(
            prefix_running, scores, visible, portion[..., HD:], "pikgn,pnkd->pikgd"
        )
    running = prefix_running
    maxima, totals, weighted = running
    attended = (
        (weighted / totals[..., None])
        .astype(jnp.bfloat16)
        .reshape(prompts * rows_dev, heads_dev * HD)
    )
    pieces = span_kv.reshape(
        prompts, rows_dev // block_rows // tp_count, tp_count, block_rows, KVH, 2 * HD
    )
    own_rows = lax.dynamic_index_in_dim(pieces, tp_index, 2, keepdims=False)
    written = lax.all_gather(own_rows, "pool", axis=1, tiled=True)
    written = written.reshape(-1, block_rows, KVH, 2 * HD)
    targets = dest_blocks.reshape(-1)
    slot_ids = pool_index * slots_dev + jnp.arange(slots_dev)
    matching = (targets[None, :] == slot_ids[:, None]).astype(jnp.int32)
    present = jnp.sum(matching, axis=1) > 0
    source = jnp.sum(matching * jnp.arange(targets.shape[0])[None, :], axis=1)
    new_pool = jnp.where(
        present[:, None, None, None], jnp.take(written, source, axis=0), prefix_pool
    )
    d_dev = residual.shape[2]
    projected = jnp.dot(attended, out_w, preferred_element_type=jnp.float32)
    summed = lax.psum(projected, "tp")
    resid_all = lax.all_gather(residual, "tp", axis=2, tiled=True).reshape(
        prompts * rows_dev, summed.shape[1]
    )
    hidden_all = (resid_all.astype(jnp.float32) + summed).astype(jnp.bfloat16)
    hidden_all = lax.optimization_barrier(hidden_all)
    widened = hidden_all.astype(jnp.float32)
    mean_square = jnp.mean(widened * widened, axis=1)
    hidden = lax.dynamic_slice_in_dim(hidden_all, tp_index * d_dev, d_dev, 1)
    own_part = hidden.astype(jnp.float32)
    normed = (
        own_part
        * lax.rsqrt(mean_square + epsilon)[:, None]
        * norm_gain.astype(jnp.float32)[None, :]
    ).astype(jnp.bfloat16)
    return (
        hidden.reshape(prompts, rows_dev, d_dev),
        normed.reshape(prompts, rows_dev, d_dev),
        new_pool,
    )


def solution(mesh):
    placed = (
        P("groups", "pool", "tp"),
        P("groups", "pool", None, None),
        P(("groups", "pool"), "tp", None, None),
        P("groups", None),
        P("groups"),
        P("groups", None),
        P("tp", None),
        P("groups", "pool", "tp"),
        P("tp"),
    )
    return jax.shard_map(
        local,
        mesh=mesh,
        in_specs=placed,
        out_specs=(
            P("groups", "pool", "tp"),
            P("groups", "pool", "tp"),
            P(("groups", "pool"), "tp", None, None),
        ),
        check_vma=False,
    )
```

profile of v0, /device:TPU:0, one launch (start us, length us, event | category | flops | bytes accessed | tf_op | source)
XLA Modules:
  0.0 704.8 jit_solution(13560602566746231394)
XLA Ops:
  10.7 2.5 gather_fusion
  13.2 1.4 broadcast_select_fusion.1
  14.9 49.0 %all-gather.10.cloned.1.call-done = bf16[48,32,8,256]{3,2,1,0:T(8,128)(2,1)} async-done(((bf16[12,32,8,256]{3,2,1,0:T(8,128)(2,1)}), bf16[48,32,8,256]{3,2,1,0:T(8,128)(2,1)}) %all-gather.10.cloned.1.call-update) | async-done | bytes 6291472 | tf_op jit(solution)/shard_map/all_gather | solution.py:87
  63.9 7.6 %copy.111 = bf16[48,32,8,256]{3,1,2,0:T(8,128)(2,1)} copy(bf16[48,32,8,256]{3,2,1,0:T(8,128)(2,1)} %all-gather.10.cloned.1.call-done) | data formatting | bytes 12582912 | tf_op jit(solution)/shard_map/all_gather | solution.py:87
  71.5 6.3 gather_fusion.1
  77.8 6.1 fusion.35
  83.9 5.4 all-to-all-start
  92.7 16.8 %all-gather.8.cloned.1.call-done = bf16[2,512,2,256]{3,1,2,0:T(8,128)(2,1)} async-done(((bf16[2,128,2,256]{3,1,2,0:T(8,128)(2,1)}), bf16[2,512,2,256]{3,1,2,0:T(8,128)(2,1)}) %all-gather.8.cloned.1.call-update) | async-done | bytes 1048592 | tf_op jit(solution)/shard_map/all_gather | solution.py:72
  109.4 5.6 fusion.34
  115.0 180.5 %all-to-all-done = bf16[48,32,4,2,256]{4,1,3,0,2:T(8,128)(2,1)} async-done(((bf16[48,32,4,2,256]{4,1,3,0,2:T(8,128)(2,1)}), bf16[48,32,4,2,256]{4,1,3,0,2:T(8,128)(2,1)}, u32[]{:S(2)}, u32[]{:S(2)}) %all-to-all-start) | async-done | bytes 6291488 | tf_op jit(solution)/shard_map/all_to_all | solution.py:89
  295.5 6.5 copy.113
  302.0 7.9 %gather_fusion.2 = bf16[48,128,2,256]{3,1,2,0:T(8,128)(2,1)} fusion(bf16[48,128,2,256]{3,1,2,0:T(8,128)(2,1)} %bitcast.164, s32[1024]{0:T(1024)S(1)} %pad_clamp_fusion.1), kind=kCustom, calls=%fused_computation.2 | custom fusion | bytes 12583104 | tf_op jit(solution)/shard_map/jit(_take)/gather | solution.py:93
  309.9 3.4 broadcast_select_fusion
  314.3 7.1 %bitcast_reduce_fusion.1 = (f32[2,128,2,8]{1,3,2,0:T(8,128)S(1)}, f32[2,2,1024,128,8]{3,2,4,1,0:T(8,128)}) fusion(pred[2,1024]{1,0:T(4,128)(4,1)S(1)} %get-tuple-element.24, bf16[2,128,2,8,128]{4,3,2,1,0:T(8,128)(2,1)S(1)} %bitcast.158, bf16[2,1024,2,256]{3,1,2,0:T(8,128)(2,1)S(1)} %bitcast.169), kind=kOutput, calls=%fused_computation.9 | convolution fusion | flops 1086320640 | bytes 18894848 | tf_op jit(solution)/shard_map/pikgd,pnkd->pikgn/dot_general | solution.py:103
  321.5 2.8 bitcast_reduce_fusion
  324.3 7.1 %bitcast_reduce_fusion.2 = (f32[2,128,2,8]{1,3,2,0:T(8,128)S(1)}, f32[2,2,1024,128,8]{3,2,4,1,0:T(8,128)}) fusion(pred[2,1024]{1,0:T(4,128)(4,1)S(1)} %get-tuple-element.23, bf16[2,128,2,8,128]{4,3,2,1,0:T(8,128)(2,1)S(1)} %bitcast.160, bf16[2,1024,2,256]{3,1,2,0:T(8,128)(2,1)S(1)} %bitcast.171), kind=kOutput, calls=%fused_computation.13 | convolution fusion | flops 1086320640 | bytes 18894848 | tf_op jit(solution)/shard_map/pikgd,pnkd->pikgn/dot_general | solution.py:103
  331.5 4.7 fusion.12
  336.2 2.1 fusion.36
  338.3 14.7 %fusion.6 = (f32[2,128,2,8]{1,3,2,0:T(8,128)S(1)}, f32[2,128,2,8]{1,3,2,0:T(8,128)S(1)}) fusion(f32[2,2,1024,128,8]{3,2,4,1,0:T(8,128)} %get-tuple-element.33, f32[2,128,2,8]{1,3,2,0:T(8,128)S(1)} %get-tuple-element.13, pred[2,1024]{1,0:T(4,128)(4,1)S(1)} %get-tuple-element.23, f32[2,128,2,8]{1,3,2,0:T(8,128)S(1)} %get-tuple-element.12, ...), kind=kLoop, calls=%fused_computation.19 | loop fusion | flops 41934848 | bytes 33624064 | tf_op jit(solution)/shard_map/reduce_sum | solution.py:25
  353.1 3.4 fusion.37
  356.5 9.7 %fusion.10 = f32[2,2,128,128,8]{3,2,4,1,0:T(8,128)} fusion(f32[2,2,1024,128,8]{3,2,4,1,0:T(8,128)} %get-tuple-element.31, f32[2,128,2,8]{1,3,2,0:T(8,128)S(1)} %get-tuple-element.12, pred[2,1024]{1,0:T(4,128)(4,1)S(1)} %get-tuple-element.24, bf16[2,1024,2,256]{3,1,2,0:T(8,128)(2,1)S(1)} %bitcast.170), kind=kOutput, calls=%fused_computation.22 | convolution fusion | flops 1090519040 | bytes 19947520 | tf_op jit(solution)/shard_map/pikgn,pnkd->pikgd/dot_general | solution.py:26
  366.1 9.7 %fusion.7 = f32[2,2,128,128,8]{3,2,4,1,0:T(8,128)} fusion(f32[2,2,1024,128,8]{3,2,4,1,0:T(8,128)} %get-tuple-element.33, f32[2,128,2,8]{1,3,2,0:T(8,128)S(1)} %get-tuple-element.13, pred[2,1024]{1,0:T(4,128)(4,1)S(1)} %get-tuple-element.23, bf16[2,1024,2,256]{3,1,2,0:T(8,128)(2,1)S(1)} %bitcast.172), kind=kOutput, calls=%fused_computation.20 | convolution fusion | flops 1090519040 | bytes 19947520 | tf_op jit(solution)/shard_map/pikgn,pnkd->pikgd/dot_general | solution.py:26
  375.8 6.6 fusion.44
  382.4 1.0 copy.126
  383.9 17.0 %fusion.90 = f32[256,8192]{1,0:T(8,128)} fusion(bf16[256,2048]{1,0:T(8,128)(2,1)S(1)} %reshape.579, bf16[2048,8192]{1,0:T(8,128)(2,1)} %param.15), kind=kOutput, calls=%fused_computation.173 | convolution fusion | flops 8589934592 | bytes 42991616 | tf_op jit(solution)/shard_map/dot_general | solution.py:137
  401.8 1.3 copy.127
  403.1 2.5 gather_fusion.3
  405.7 5.0 select_select_fusion
  410.7 279.4 %all-reduce.2.cloned.1.call-done = f32[256,8192]{1,0:T(8,128)} async-done(((f32[256,8192]{1,0:T(8,128)}), f32[256,8192]{1,0:T(8,128)}) %all-reduce.2.cloned.1.call-update) | async-done | bytes 8388624 | tf_op jit(solution)/shard_map/psum | solution.py:138
  690.1 5.7 fusion.15
  695.8 0.9 multiply_reduce_fusion
  696.7 1.6 multiply_convert_fusion
  (88 shorter events, 9.4 us)
Async XLA Ops:
  7.2 82.2 %copy-start = (bf16[2,128,8,256]{3,2,1,0:T(8,128)(2,1)S(1)}, bf16[2,128,8,256]{3,2,1,0:T(8,128)(2,1)}, u32[]{:S(2)}) copy-start(bf16[2,128,8,256]{3,2,1,0:T(8,128)(2,1)} %param.10) | copy-start | bytes 3145732
  7.2 56.7 %all-gather.10.cloned.1.call-start = ((), (), s32[]{:S(2)}) async-start(), calls=%async_computation.3 | async-start | bytes 7864320 | tf_op jit(solution)/shard_map/all_gather | solution.py:87
  83.9 8.2 %copy-start.2 = (bf16[2,128,2048]{2,1,0:T(8,128)(2,1)S(1)}, bf16[2,128,2048]{2,1,0:T(8,128)(2,1)}, u32[]{:S(2)}) copy-start(bf16[2,128,2048]{2,1,0:T(8,128)(2,1)} %param.9) | copy-start | bytes 3145732
  83.9 8.4 %copy-start.5 = (s32[2,24]{1,0:T(2,128)S(1)}, s32[2,24]{1,0:T(2,128)}, u32[]{:S(2)}) copy-start(s32[2,24]{1,0:T(2,128)} %param.12) | copy-start | bytes 580
  83.9 8.4 %copy-start.6 = (s32[2]{0:T(128)S(1)}, s32[2]{0:T(128)}, u32[]{:S(2)}) copy-start(s32[2]{0:T(128)} %param.13) | copy-start | bytes 28
  83.9 211.6 %all-to-all-start = ((bf16[48,32,4,2,256]{4,1,3,0,2:T(8,128)(2,1)}), bf16[48,32,4,2,256]{4,1,3,0,2:T(8,128)(2,1)}, u32[]{:S(2)}, u32[]{:S(2)}) async-start(bf16[48,32,4,2,256]{4,1,3,0,2:T(8,128)(2,1)} %fusion.35), calls=%async_computation | async-start | bytes 12582912 | tf_op jit(solution)/shard_map/all_to_all | solution.py:89
  89.3 20.2 %all-gather.8.cloned.1.call-start = ((), (), s32[]{:S(2)}) async-start(), calls=%async_computation.2 | async-start | bytes 1310720 | tf_op jit(solution)/shard_map/all_gather | solution.py:72
  90.4 311.5 %all-gather.12.cloned.1.call-start = ((), (), s32[]{:S(2)}) async-start(), calls=%async_computation.5 | async-start | bytes 1310720 | tf_op jit(solution)/shard_map/all_gather | solution.py:126
  91.2 319.5 %all-gather.6.cloned.1.call-start = ((), (), s32[]{:S(2)}) async-start(), calls=%async_computation.1 | async-start | bytes 5242880 | tf_op jit(solution)/shard_map/all_gather | solution.py:139
  91.8 598.3 %all-reduce.2.cloned.1.call-start = ((), (), s32[]{:S(2)}) async-start(), calls=%async_computation.4 | async-start | bytes 16777216 | tf_op jit(solution)/shard_map/psum | solution.py:138
  321.5 14.7 %slice-start = ((s8[8388608]{0:T(1024)(128)(4,1)}), s8[4194304]{0:T(1024)(128)(4,1)S(1)}, s32[]{:S(2)}) async-start(s8[8388608]{0:T(1024)(128)(4,1)} %bitcast.161), calls=%async_computation.6 | async-start | bytes 8388608
  324.3 11.9 %slice-start.1 = ((s8[8388608]{0:T(1024)(128)(4,1)}), s8[4194304]{0:T(1024)(128)(4,1)S(1)}, s32[]{:S(2)}) async-start(s8[8388608]{0:T(1024)(128)(4,1)} %bitcast.161), calls=%async_computation.7 | async-start | bytes 8388608
  338.3 14.7 %copy-start.3 = (bf16[2,512,2,256]{3,1,2,0:T(8,128)(2,1)S(1)}, bf16[2,512,2,256]{3,1,2,0:T(8,128)(2,1)}, u32[]{:S(2)}) copy-start(bf16[2,512,2,256]{3,1,2,0:T(8,128)(2,1)} %all-gather.8.cloned.1.call-done) | copy-start | bytes 3145732
  400.9 0.7 copy-start.4
  400.9 0.7 copy-start.7
  405.7 292.7 %copy-start.1 = (bf16[2,128,8,256]{3,2,1,0:T(8,128)(2,1)S(1)}, bf16[2,128,8,256]{3,2,1,0:T(8,128)(2,1)}, u32[]{:S(2)}) copy-start(bf16[2,128,8,256]{3,2,1,0:T(8,128)(2,1)} %param.10) | copy-start | bytes 3145732
Sparse Core Ops, SparseCore 0:
  14.8 49.0 all-gather.9
  92.2 17.1 all-gather.7
  111.6 16.7 all-gather.11
  129.8 147.8 all-gather.5
  401.1 288.9 all-reduce.1
where the time goes:
time: 706 us; the launch traced here: 705 us
  waiting for transfers between devices  526 us (75%)
  matrix products  69.1 us (10%)
  other arithmetic  49 us (7%)
  local copies, waits for them, and re-layouts  40.8 us (6%)
  between operations  14.1 us (2%)
    psum x1, waiting for transfers between devices, local(): summed = lax.psum(projected, 'tp')  279 us
    all_to_all x1, waiting for transfers between devices, local(): lax.all_to_all(outgoing, 'tp', split_axis=2, concat_axis=1, tiled=True)  180 us
    all_gather x1, waiting for transfers between devices, local(): everyone = lax.all_gather(held_blocks, 'pool', axis=0, tiled=True)  49 us
    dot_general x4, matrix products, online_update(): jnp.einsum(pattern, weights, values.astype(jnp.float32))  29.4 us
    reduce_sum x3, other arithmetic, online_update(): totals = totals * factor + jnp.sum(weights, axis=-1)  21.5 us
    dot_general x3, matrix products, local(): jnp.einsum('pikgd,pnkd->pikgn', query_grid, portion[..., :HD], preferred_...  17.1 us
    dot_general x1, matrix products, local(): projected = jnp.dot(attended, out_w, preferred_element_type=jnp.float32)  17 us
    all_gather x1, waiting for transfers between devices, local(): span_portion = lax.all_gather(span_heads, 'pool', axis=1, tiled=True)  16.8 us
  transfers between devices with their start and end apart: 6, of which 4 were waited for; matrix products, arithmetic and copies ran while one was open for 17% of the time, Pallas kernels for 0%

commit v1 on v0

v1 whole, which is shorter than its diff:
```python
import functools
import math

import jax
import jax.numpy as jnp
from jax import lax
from jax.experimental import pallas as pl
from jax.experimental.pallas import tpu as pltpu
from jax.sharding import PartitionSpec as P

QH = 64
KVH = 8
HD = 128
MAXB = 24
MOST = 12

epsilon = 1e-05
lowest = -1e30
exponent_scale = math.log2(math.e) / math.sqrt(HD)
VMEM_LIMIT = 56 * 1024 * 1024

SMEM = functools.partial(pl.BlockSpec, memory_space=pltpu.SMEM)
VMEM = functools.partial(pl.BlockSpec, memory_space=pltpu.VMEM)
ANY = functools.partial(pl.BlockSpec, memory_space=pl.ANY)


def holder_of(relative, pool_index, pool_count):
    chips = pool_count // 2
    chip = lax.rem(pool_index // 2 + chips - relative // 2, chips)
    core = lax.rem(lax.rem(pool_index, 2) + relative % 2, 2)
    return chip * 2 + core


def prepare_kernel(
    tp_count, pool_count, heads_dev, hit, lens, place, pool, span, *refs
):
    counts = refs[0]
    sends = refs[1 : 1 + tp_count]
    span_out = refs[1 + tp_count]
    own_slots, held, wide, sems = refs[2 + tp_count :]
    prompts, rows_dev = span.shape[:2]
    slots_dev, block_rows = pool.shape[:2]
    kv_dev = span_out.shape[0]
    sharing = QH // KVH
    pool_index = place[0]
    tp_index = place[1]
    for slot in range(MOST):
        own_slots[slot] = 0
    own_slots[MOST] = 0
    for prompt in range(prompts):
        for relative in range(pool_count):
            counts[prompt, relative] = 0

        def entry(position, carry, prompt=prompt):
            block = hit[prompt, position]
            holder = block // slots_dev
            chips = pool_count // 2
            chip_away = lax.rem(pool_index // 2 + chips - holder // 2, chips)
            core_away = lax.rem(lax.rem(pool_index, 2) + lax.rem(holder, 2), 2)
            relative = chip_away * 2 + core_away
            counts[prompt, relative] = counts[prompt, relative] + 1

            @pl.when(holder == pool_index)
            def _():
                rank = own_slots[MOST]
                own_slots[rank] = block - holder * slots_dev
                own_slots[MOST] = rank + 1

            return carry

        lax.fori_loop(0, lens[prompt], entry, 0)
    copies = []
    for slot in range(MOST):
        copy = pltpu.make_async_copy(pool.at[own_slots[slot]], held.at[slot], sems.at[slot])
        copy.start()
        copies.append(copy)

    def first_head(shift):
        device = lax.rem(tp_index + shift, tp_count)
        return device * heads_dev // sharing

    def spread(block, rows):
        for half in range(2):
            wide[half, pl.ds(0, rows * KVH), :] = (
                block[:, :, half * HD : (half + 1) * HD].astype(jnp.float32).reshape(rows * KVH, HD)
            )

    def one_head(head, rows):
        here = pl.ds(head, rows, stride=KVH)
        return jnp.concatenate([wide[half, here, :] for half in range(2)], axis=1).astype(
            jnp.bfloat16
        )

    for prompt in range(prompts):
        spread(span[prompt], rows_dev)
        for head in range(kv_dev):
            span_out[head, prompt] = one_head(first_head(0) + head, rows_dev)
    for slot in range(MOST):
        copies[slot].wait()
        spread(held[slot], block_rows)
        for shift in range(tp_count):
            for head in range(kv_dev):
                sends[shift][slot, head] = one_head(first_head(shift) + head, block_rows)


def prepare(tp_count, pool_count, heads_dev, kv_dev, hit, lens, place, pool, span):
    prompts, rows_dev = span.shape[:2]
    block_rows = pool.shape[1]
    send = jax.ShapeDtypeStruct((MOST, kv_dev, block_rows, 2 * HD), jnp.bfloat16)
    outs = pl.pallas_call(
        functools.partial(prepare_kernel, tp_count, pool_count, heads_dev),
        out_shape=[jax.ShapeDtypeStruct((prompts, pool_count), jnp.int32)]
        + [send] * tp_count
        + [jax.ShapeDtypeStruct((kv_dev, prompts, rows_dev, 2 * HD), jnp.bfloat16)],
        in_specs=[SMEM(), SMEM(), SMEM(), ANY(), VMEM()],
        out_specs=[SMEM()] + [VMEM()] * (tp_count + 1),
        scratch_shapes=[
            pltpu.SMEM((MOST + 1,), jnp.int32),
            pltpu.VMEM((MOST, block_rows, KVH, 2 * HD), jnp.bfloat16),
            pltpu.VMEM((2, max(rows_dev, block_rows) * KVH, HD), jnp.float32),
            pltpu.SemaphoreType.DMA((MOST,)),
        ],
        compiler_params=pltpu.CompilerParams(vmem_limit_bytes=VMEM_LIMIT),
        cost_estimate=pl.CostEstimate(flops=0, bytes_accessed=8 << 20, transcendentals=0),
        name="prepare",
    )(hit, lens, place, pool, span)
    return outs[0], outs[1 : 1 + tp_count], outs[1 + tp_count]


def attend_kernel(
    n_chunks, pool_count, with_span, with_state, final, block_heads, place, lens, counts, query, *refs
):
    refs = list(refs)
    chunk_refs = [[refs.pop(0) for _ in range(pool_count)] for _ in range(n_chunks)]
    span_refs = [refs.pop(0) for _ in range(pool_count)] if with_span else []
    state_in = [refs.pop(0) for _ in range(3)] if with_state else None
    outs = [refs.pop(0) for _ in range(1 if final else 3)]
    keys, valued = refs[:2]
    span_keys, span_valued = refs[2:4] if with_span else (None, None)
    prompt = pl.program_id(1)
    pool_index = place[0]
    rows_dev = query.shape[1]
    block_rows = chunk_refs[0][0].shape[2]
    group = query.shape[2] // HD
    held = keys.dtype

    starts = []
    for relative in range(pool_count):
        start = jnp.int32(0)
        for other in range(counts.shape[0]):
            start += jnp.where(other < prompt, counts[other, relative], 0)
        starts.append(start)
    for chunk in range(n_chunks):
        offset = jnp.int32(0)
        for relative in range(pool_count):
            source = chunk_refs[chunk][relative]

            def bring(index, carry, source=source, offset=offset, start=starts[relative]):
                block = source[start + index, 0].astype(held)
                place_at = pl.ds(pl.multiple_of((offset + index) * block_rows, block_rows), block_rows)
                keys[chunk, place_at, :] = block[:, :HD]
                valued[chunk, place_at, :HD] = block[:, HD:]
                valued[chunk, place_at, HD:] = jnp.ones((block_rows, HD), held)
                return carry

            count = counts[prompt, relative]
            lax.fori_loop(0, count, bring, 0)
            offset += count

        def fill(index, carry):
            place_at = pl.ds(pl.multiple_of(index * block_rows, block_rows), block_rows)
            keys[chunk, place_at, :] = keys[chunk, pl.ds(0, block_rows), :]
            valued[chunk, place_at, :] = jnp.zeros((block_rows, 2 * HD), held)
            return carry

        lax.fori_loop(offset, MAXB, fill, 0)
    if with_span:
        for relative in range(pool_count):
            block = span_refs[relative][0, 0]
            place_at = pl.ds(relative * rows_dev, rows_dev)
            span_keys[place_at, :] = block[:, :HD]
            span_valued[place_at, :HD] = block[:, HD:]
            span_valued[place_at, HD:] = jnp.ones((rows_dev, HD), jnp.bfloat16)

    rows = block_heads * rows_dev
    for first in range(0, group, block_heads):
        heads = range(first, first + block_heads)
        here = pl.ds(first * rows_dev, rows)
        asked = jnp.concatenate([query[0, :, h * HD : (h + 1) * HD] for h in heads], axis=0)
        running = None
        if with_state:
            running = [ref[0, 0, here, :] for ref in state_in]

        def update(running, scores, valued_here):
            peak = jnp.max(scores, axis=1, keepdims=True)
            if running is None:
                new_peak = jnp.broadcast_to(peak, (rows, HD))
            else:
                new_peak = jnp.maximum(running[0], peak)
            weights = jnp.exp2((scores - new_peak[:, :1]) * exponent_scale).astype(jnp.bfloat16)
            result = jnp.dot(weights, valued_here, preferred_element_type=jnp.float32)
            if running is None:
                return [new_peak, result[:, HD:], result[:, :HD]]
            factor = jnp.exp2((running[0] - new_peak) * exponent_scale)
            return [
                new_peak,
                running[1] * factor + result[:, HD:],
                running[2] * factor + result[:, :HD],
            ]

        def score(keys_here):
            return lax.dot_general(
                asked, keys_here, (((1,), (1,)), ((), ())), preferred_element_type=jnp.float32
            )

        if with_span:
            scores = score(span_keys[...])
            columns = lax.broadcasted_iota(jnp.int32, (1, rows_dev), 1)
            key_pos = jnp.concatenate(
                [
                    holder_of(relative, pool_index, pool_count) * rows_dev + columns
                    for relative in range(pool_count)
                ],
                axis=1,
            )
            query_pos = pool_index * rows_dev + lax.rem(
                lax.broadcasted_iota(jnp.int32, (rows, 1), 0), rows_dev
            )
            running = update(
                running, jnp.where(key_pos <= query_pos, scores, lowest), span_valued[...]
            )
        for chunk in range(n_chunks):
            running = update(
                running,
                score(keys[chunk].astype(jnp.bfloat16)),
                valued[chunk].astype(jnp.bfloat16),
            )
        if final:
            attended = (running[2] / running[1]).astype(jnp.bfloat16)
            for at, h in enumerate(heads):
                outs[0][0, :, h * HD : (h + 1) * HD] = attended[at * rows_dev : (at + 1) * rows_dev]
        else:
            for ref, value in zip(outs, running):
                ref[0, 0, here, :] = value


def attend(place, lens, counts, queries, chunks, kv_dev, span=None, state=None, final=False):
    pool_count = len(chunks[0])
    prompts, rows_dev, features = queries.shape
    group = features // HD // kv_dev
    block_rows = chunks[0][0].shape[2]
    key_rows = MAXB * block_rows
    held = jnp.bfloat16 if block_rows % 16 == 0 else jnp.float32
    block_heads = min(2, group)
    query_spec = pl.BlockSpec((1, rows_dev, group * HD), lambda k, p: (p, 0, k))
    chunk_spec = pl.BlockSpec((MOST, 1, block_rows, 2 * HD), lambda k, p: (0, k, 0, 0))
    span_spec = pl.BlockSpec((1, 1, rows_dev, 2 * HD), lambda k, p: (k, p, 0, 0))
    state_spec = pl.BlockSpec((1, 1, group * rows_dev, HD), lambda k, p: (k, p, 0, 0))
    state_shape = jax.ShapeDtypeStruct((kv_dev, prompts, group * rows_dev, HD), jnp.float32)
    operands = [place, lens, counts, queries] + [a for chunk in chunks for a in chunk]
    specs = [SMEM(), SMEM(), SMEM(), query_spec] + [chunk_spec] * (pool_count * len(chunks))
    scratch = [
        pltpu.VMEM((len(chunks), key_rows, HD), held),
        pltpu.VMEM((len(chunks), key_rows, 2 * HD), held),
    ]
    n_keys = key_rows * len(chunks)
    if span is not None:
        operands += span
        specs += [span_spec] * pool_count
        scratch += [
            pltpu.VMEM((pool_count * rows_dev, HD), jnp.bfloat16),
            pltpu.VMEM((pool_count * rows_dev, 2 * HD), jnp.bfloat16),
        ]
        n_keys += pool_count * rows_dev
    if state is not None:
        operands += state
        specs += [state_spec] * 3
    if final:
        out_shape = [jax.ShapeDtypeStruct(queries.shape, jnp.bfloat16)]
        out_specs = [query_spec]
    else:
        out_shape = [state_shape] * 3
        out_specs = [state_spec] * 3
    rows = prompts * rows_dev * kv_dev * group
    return pl.pallas_call(
        functools.partial(
            attend_kernel,
            len(chunks),
            pool_count,
            span is not None,
            state is not None,
            final,
            block_heads,
        ),
        grid=(kv_dev, prompts),
        out_shape=out_shape,
        in_specs=specs,
        out_specs=out_specs,
        scratch_shapes=scratch,
        compiler_params=pltpu.CompilerParams(vmem_limit_bytes=VMEM_LIMIT),
        cost_estimate=pl.CostEstimate(
            flops=rows * n_keys * HD * 6,
            bytes_accessed=8 << 20,
            transcendentals=rows * n_keys,
        ),
        name="attend",
    )(*operands)


def project_kernel(which, attended, weight, out):
    out[...] = jnp.dot(
        attended[...], weight[...], preferred_element_type=jnp.float32
    ).astype(out.dtype)


def project(which, attended, out_w, width, dtype):
    rows, depth = attended.shape
    tile = min(512, width)
    steps = width // tile
    return pl.pallas_call(
        project_kernel,
        grid_spec=pltpu.PrefetchScalarGridSpec(
            num_scalar_prefetch=1,
            grid=(steps,),
            in_specs=[
                pl.BlockSpec((rows, depth), lambda j, which: (0, 0)),
                pl.BlockSpec((depth, tile), lambda j, which: (0, which[0] * steps + j)),
            ],
            out_specs=pl.BlockSpec((rows, tile), lambda j, which: (0, j)),
        ),
        out_shape=jax.ShapeDtypeStruct((rows, width), dtype),
        compiler_params=pltpu.CompilerParams(vmem_limit_bytes=VMEM_LIMIT),
        cost_estimate=pl.CostEstimate(
            flops=2 * rows * depth * width,
            bytes_accessed=2 * depth * width + 4 * rows * width,
            transcendentals=0,
        ),
        name="project",
    )(which.reshape(1), attended, out_w)


def over_pool(array, pool_count):
    gathered = []
    swap = [(i, i ^ 1) for i in range(pool_count)]
    for chips in range(pool_count // 2):
        pairs = [(i, (i + 2 * chips) % pool_count) for i in range(pool_count)]
        arrived = array if chips == 0 else lax.ppermute(array, "pool", pairs)
        gathered += [arrived, lax.ppermute(arrived, "pool", swap)]
    return gathered


def local(
    queries, span_kv, prefix_pool, hit_blocks, prefix_len, dest_blocks, out_w, residual, norm_gain
):
    tp_count = lax.axis_size("tp")
    tp_index = lax.axis_index("tp")
    pool_count = lax.axis_size("pool")
    pool_index = lax.axis_index("pool")
    prompts, rows_dev = queries.shape[:2]
    heads_dev = queries.shape[2] // HD
    kv_dev = max(1, heads_dev // (QH // KVH))
    slots_dev, block_rows = prefix_pool.shape[:2]
    d_dev = residual.shape[2]
    place = jnp.stack([pool_index, tp_index]).astype(jnp.int32)

    counts, sends, span_own = prepare(
        tp_count, pool_count, heads_dev, kv_dev, hit_blocks, prefix_len, place, prefix_pool, span_kv
    )
    chunks = [over_pool(sends[0], pool_count)]
    span = over_pool(span_own, pool_count)
    order = sorted(range(1, tp_count), key=lambda s: min(s, tp_count - s))
    for shift in order:
        pairs = [(i, (i + shift) % tp_count) for i in range(tp_count)]
        chunks.append(over_pool(lax.ppermute(sends[shift], "tp", pairs), pool_count))
    state = attend(place, prefix_len, counts, queries, chunks[:-1], kv_dev, span=span)
    attended = attend(
        place, prefix_len, counts, queries, chunks[-1:], kv_dev, state=state, final=True
    )[0]
    attended = attended.reshape(prompts * rows_dev, heads_dev * HD)

    last = tp_count - 1
    from_left = from_right = None
    for step in range(1, tp_count):
        right_pairs = [(i, i + 1) for i in range(last) if step >= i + 1]
        left_pairs = [(i, i - 1) for i in range(1, tp_count) if step >= tp_count - i]
        to_right = lax.rem(tp_index + tp_count - step, tp_count)
        to_left = lax.rem(tp_index + step, tp_count)
        right_sources = {i for i, _ in right_pairs}
        if right_sources & {i for i, _ in left_pairs}:
            right = project(to_right, attended, out_w, d_dev, jnp.float32)
            left = project(to_left, attended, out_w, d_dev, jnp.float32)
        else:
            cut = max(right_sources)
            which = jnp.where(tp_index <= cut, to_right, to_left)
            first = jnp.bfloat16 if step == 1 else jnp.float32
            right = left = project(which, attended, out_w, d_dev, first)
        parts = []
        for prompt in range(prompts):
            these = slice(prompt * rows_dev, (prompt + 1) * rows_dev)
            going = [right[these], left[these]]
            if step > 1:
                going = [
                    (mine + came[prompt].astype(jnp.float32)).astype(jnp.bfloat16)
                    for mine, came in zip(going, (from_left, from_right))
                ]
            parts.append(
                (lax.ppermute(going[0], "tp", right_pairs), lax.ppermute(going[1], "tp", left_pairs))
            )
        from_left = [part[0] for part in parts]
        from_right = [part[1] for part in parts]
    own = project(tp_index, attended, out_w, d_dev, jnp.float32)
    own = own.reshape(prompts, rows_dev, d_dev) + residual.astype(jnp.float32)

    pieces = span_kv.reshape(
        prompts, rows_dev // block_rows // tp_count, tp_count, block_rows, KVH, 2 * HD
    )
    own_rows = lax.dynamic_index_in_dim(pieces, tp_index, 2, keepdims=False)
    written = lax.all_gather(own_rows, "pool", axis=1, tiled=True)
    written = written.reshape(-1, block_rows, KVH, 2 * HD)
    targets = dest_blocks.reshape(-1)
    slot_ids = pool_index * slots_dev + jnp.arange(slots_dev)
    matching = (targets[None, :] == slot_ids[:, None]).astype(jnp.int32)
    present = jnp.sum(matching, axis=1) > 0
    source = jnp.sum(matching * jnp.arange(targets.shape[0])[None, :], axis=1)
    new_pool = jnp.where(
        present[:, None, None, None], jnp.take(written, source, axis=0), prefix_pool
    )

    hidden = jnp.stack(
        [
            (
                own[prompt]
                + from_left[prompt].astype(jnp.float32)
                + from_right[prompt].astype(jnp.float32)
            ).astype(jnp.bfloat16)
            for prompt in range(prompts)
        ]
    )
    hidden = lax.optimization_barrier(hidden)
    widened = hidden.astype(jnp.float32)
    squares = jnp.sum(widened * widened, axis=2)
    total = squares
    for shift in range(1, tp_count):
        pairs = [(i, (i + shift) % tp_count) for i in range(tp_count)]
        total = total + lax.ppermute(squares, "tp", pairs)
    mean_square = total / (d_dev * tp_count)
    normed = (
        widened
        * lax.rsqrt(mean_square + epsilon)[..., None]
        * norm_gain.astype(jnp.float32)[None, None, :]
    ).astype(jnp.bfloat16)
    return hidden, normed, new_pool


def solution(mesh):
    placed = (
        P("groups", "pool", "tp"),
        P("groups", "pool", None, None),
        P(("groups", "pool"), "tp", None, None),
        P("groups", None),
        P("groups"),
        P("groups", None),
        P("tp", None),
        P("groups", "pool", "tp"),
        P("tp"),
    )
    return jax.shard_map(
        local,
        mesh=mesh,
        in_specs=placed,
        out_specs=(
            P("groups", "pool", "tp"),
            P("groups", "pool", "tp"),
            P(("groups", "pool"), "tp", None, None),
        ),
        check_vma=False,
    )
```

time: 706 us -> 240 us (0.34)
  waiting for transfers between devices: 526 us -> 87 us
  Pallas kernels: 0 us -> 72.5 us
  matrix products: 69.1 us -> 0 us
  starting transfers between devices: 5.57 us -> 45 us
  other arithmetic: 49 us -> 11.6 us
  local copies, waits for them, and re-layouts: 40.8 us -> 8.15 us
    psum x1 -> x0, waiting for transfers between devices: 279 us -> none  [local(): summed = lax.psum(projected, 'tp')]
    all_to_all x1 -> x0, waiting for transfers between devices: 180 us -> none  [local(): lax.all_to_all(outgoing, 'tp', split_axis=2, concat_axis=1, tiled=True)]
    ppermute x0 -> x33, waiting for transfers between devices: none -> 87 us  [the longest x3 24.2 us: local(): lax.ppermute(sends[shift], 'tp', pairs)]
    pallas_call x0 -> x8, Pallas kernels: none -> 72.5 us  [the longest x5 34.1 us: project(): pl.pallas_call(project_kernel, grid_spec=pltpu.PrefetchScalarGridSpec(num...]
    dot_general x9 -> x0, matrix products: 69.1 us -> none  [the longest x4 29.4 us: online_update(): jnp.einsum(pattern, weights, values.astype(jnp.float32))]
    all_gather x3 -> x0, waiting for transfers between devices: 65.7 us -> none  [the longest x1 49 us: local(): everyone = lax.all_gather(held_blocks, 'pool', axis=0, tiled=True)]
    ppermute x0 -> x33, starting transfers between devices: none -> 44.9 us  [the longest x6 21.3 us: local(): lax.ppermute(going[0], 'tp', right_pairs)]
    reduce_sum x6 -> x1, other arithmetic: 22.9 us -> 0.29 us  [local(): squares = jnp.sum(widened * widened, axis=2)]
  transfers between devices with their start and end apart: 6 -> 34, of which waited for: 4 -> 10; matrix products, arithmetic and copies ran while one was open for 17% -> 6% of each run, Pallas kernels for 0% -> 28%
where the time goes in v1:
time: 240 us; the launch traced here: 239 us
  waiting for transfers between devices  87 us (36%)
  Pallas kernels  72.5 us (30%)
  starting transfers between devices  45 us (19%)
  between operations  14.5 us (6%)
  other arithmetic  11.6 us (5%)
  local copies, waits for them, and re-layouts  8.15 us (3%)
    pallas_call x5, Pallas kernels, project(): pl.pallas_call(project_kernel, grid_spec=pltpu.PrefetchScalarGridSpec(num...  34.1 us
    pallas_call x2, Pallas kernels, attend(): pl.pallas_call(functools.partial(attend_kernel, len(chunks), pool_count,...  33.1 us
    ppermute x3, waiting for transfers between devices, local(): lax.ppermute(sends[shift], 'tp', pairs)  24.2 us
    ppermute x6, waiting for transfers between devices, local(): lax.ppermute(going[1], 'tp', left_pairs)  23.5 us
    ppermute x6, waiting for transfers between devices, local(): lax.ppermute(going[0], 'tp', right_pairs)  21.6 us
    ppermute x6, starting transfers between devices, local(): lax.ppermute(going[0], 'tp', right_pairs)  21.3 us
    ppermute x5, waiting for transfers between devices, over_pool(): arrived = array if chips == 0 else lax.ppermute(array, 'pool', pairs)  17.6 us
    ppermute x3, starting transfers between devices, local(): lax.ppermute(sends[shift], 'tp', pairs)  7.11 us
  transfers between devices with their start and end apart: 34, of which 10 were waited for; matrix products, arithmetic and copies ran while one was open for 6% of the time, Pallas kernels for 28%

profile of v1, /device:TPU:0, one launch (start us, length us, event | category | flops | bytes accessed | tf_op | source)
XLA Modules:
  0.0 238.7 jit_solution(18026543082790451756)
XLA Ops:
  7.9 5.4 %prepare.1 = (s32[2,4]{1,0:T(2,128)}, bf16[12,2,32,256]{3,2,1,0:T(8,128)(2,1)}, bf16[12,2,32,256]{3,2,1,0:T(8,128)(2,1)}, bf16[12,2,32,256]{3,2,1,0:T(8,128)(2,1...) custom-call(s32[2,24]{1,0:T(2,128)} %hit.1, s32[2]{0:T(128)} %lens.5, s32[2]{0:T(128)} %pad_add_fusion.place, ...), custom_call_target="tpu_custom_call" | custom-call | bytes 8388608 | tf_op jit(solution)/shard_map/prepare/pallas_call | solution.py:110
  13.2 3.0 %collective-permute-start.16 = (bf16[2,2,128,256]{3,2,1,0:T(8,128)(2,1)}, bf16[2,2,128,256]{3,2,1,0:T(8,128)(2,1)S(1)}, u32[]{:S(2)}, u32[]{:S(2)}) collective-permute-start(bf16[2,2,128,256]{3,2,1,0:T(8,128)(2,1)} %get-tuple-element.17.refs_12_), channel_id=1, source_target_pairs={{0,8},{4,12},{8,0},{12,4},{1,9},{5,13},{9,1},{13,5},{2,10},{6,14},... | collective-permute-start | bytes 786440 | tf_op jit(solution)/shard_map/ppermute | solution.py:347
  17.8 2.2 collective-permute-start.11
  20.4 3.1 %collective-permute-done.16.refs_14_ = bf16[2,2,128,256]{3,2,1,0:T(8,128)(2,1)S(1)} collective-permute-done((bf16[2,2,128,256]{3,2,1,0:T(8,128)(2,1)}, bf16[2,2,128,256]{3,2,1,0:T(8,128)(2,1)S(1)}, u32[]{:S(2)}, u32[]{:S(2)}) %collective-permute-start.16) | collective-permute-done | bytes 262176 | tf_op jit(solution)/shard_map/ppermute | solution.py:347
  23.5 3.3 %collective-permute-start = (bf16[12,2,32,256]{3,2,1,0:T(8,128)(2,1)}, bf16[12,2,32,256]{3,2,1,0:T(8,128)(2,1)S(1)}, u32[]{:S(2)}, u32[]{:S(2)}) collective-permute-start(bf16[12,2,32,256]{3,2,1,0:T(8,128)(2,1)} %get-tuple-element.13), channel_id=1, source_target_pairs={{0,2},{1,3},{2,0},{3,1},{4,6},{5,7},{6,4},{7,5},{8,10},{9,11},{10,... | collective-permute-start | bytes 1179656 | tf_op jit(solution)/shard_map/ppermute | solution.py:374
  26.8 3.5 %collective-permute-done.7.refs_4_ = bf16[12,2,32,256]{3,2,1,0:T(8,128)(2,1)S(1)} collective-permute-done((bf16[12,2,32,256]{3,2,1,0:T(8,128)(2,1)}, bf16[12,2,32,256]{3,2,1,0:T(8,128)(2,1)S(1)}, u32[]{:S(2)}, u32[]{:S(2)}) %collective-permute-start.7) | collective-permute-done | bytes 393248 | tf_op jit(solution)/shard_map/ppermute | solution.py:374
  30.6 6.1 %collective-permute-done.11.refs_8_ = bf16[12,2,32,256]{3,2,1,0:T(8,128)(2,1)S(1)} collective-permute-done((bf16[12,2,32,256]{3,2,1,0:T(8,128)(2,1)}, bf16[12,2,32,256]{3,2,1,0:T(8,128)(2,1)S(1)}, u32[]{:S(2)}, u32[]{:S(2)}) %collective-permute-start.11) | collective-permute-done | bytes 393248 | tf_op jit(solution)/shard_map/ppermute | solution.py:374
  37.9 1.7 constant_dynamic-slice_fusion
  39.6 14.6 %collective-permute-done.refs_0_ = bf16[12,2,32,256]{3,2,1,0:T(8,128)(2,1)S(1)} collective-permute-done((bf16[12,2,32,256]{3,2,1,0:T(8,128)(2,1)}, bf16[12,2,32,256]{3,2,1,0:T(8,128)(2,1)S(1)}, u32[]{:S(2)}, u32[]{:S(2)}) %collective-permute-start) | collective-permute-done | bytes 393248 | tf_op jit(solution)/shard_map/ppermute | solution.py:374
  56.9 14.4 %collective-permute-done.2.refs_2_ = bf16[12,2,32,256]{3,2,1,0:T(8,128)(2,1)S(1)} collective-permute-done((bf16[12,2,32,256]{3,2,1,0:T(8,128)(2,1)S(1)}, bf16[12,2,32,256]{3,2,1,0:T(8,128)(2,1)S(1)}, u32[]{:S(2)}, u32[]{:S(2)}) %collective-permute-start.2) | collective-permute-done | bytes 393248 | tf_op jit(solution)/shard_map/ppermute | solution.py:347
  71.4 23.2 %attend.2 = (f32[2,2,1024,128]{3,2,1,0:T(8,128)}, f32[2,2,1024,128]{3,2,1,0:T(8,128)}, f32[2,2,1024,128]{3,2,1,0:T(8,128)}) custom-call(s32[2]{0:T(128)} %pad_add_fusion.place, s32[2]{0:T(128)} %lens.5, s32[2,4]{1,0:T(2,128)} %get-tuple-element.12.counts, bf16[2,128,2048]{2,1,0:T(8,128)(2,1)} %query.3, bf16[12,2,32,256]{3,2,1,0:T(8,128)(2,1)} %get-tuple-element.14.refs_0_, ...), custom_call_target="tpu_custom_call" | custom-call | flops 8858370048 | bytes 8388608 | tf_op jit(solution)/shard_map/attend/pallas_call | solution.py:285
  95.6 9.8 %attend.3 = bf16[2,128,2048]{2,1,0:T(8,128)(2,1)} custom-call(s32[2]{0:T(128)} %pad_add_fusion.place, s32[2]{0:T(128)} %lens.5, s32[2,4]{1,0:T(2,128)} %get-tuple-element.12.counts, bf16[2,128,2048]{2,1,0:T(8,128)(2,1)} %query.3, bf16[12,2,32,256]{3,2,1,0:T(8,128)(2,1)} %copy-done.7, bf16[12,2,32,256]{3,2,1,0:T(8,128)(2,1)} %copy-done.9, ...), custom_call_target="tpu_custom_call" | custom-call | flops 2415919104 | bytes 8388608 | tf_op jit(solution)/shard_map/attend/pallas_call | solution.py:285
  105.4 6.6 %project.8 = bf16[256,2048]{1,0:T(8,128)(2,1)} custom-call(s32[1]{0:T(128)} %bitcast.7.which, bf16[256,2048]{1,0:T(8,128)(2,1)} %bitcast.38, bf16[2048,8192]{1,0:T(8,128)(2,1)} %weight.9), custom_call_target="tpu_custom_call" | custom-call | flops 2147483648 | bytes 10485760 | tf_op jit(solution)/shard_map/project/pallas_call | solution.py:320
  117.4 6.8 %project.7 = f32[256,2048]{1,0:T(8,128)} custom-call(s32[1]{0:T(128)} %bitcast.6.which, bf16[256,2048]{1,0:T(8,128)(2,1)} %bitcast.39, bf16[2048,8192]{1,0:T(8,128)(2,1)} %weight.9), custom_call_target="tpu_custom_call" | custom-call | flops 2147483648 | bytes 10485760 | tf_op jit(solution)/shard_map/project/pallas_call | solution.py:320
  124.2 2.7 %collective-permute-done.18 = bf16[128,2048]{1,0:T(8,128)(2,1)S(1)} collective-permute-done((bf16[128,2048]{1,0:T(8,128)(2,1)S(1)}, bf16[128,2048]{1,0:T(8,128)(2,1)S(1)}, u32[]{:S(2)}, u32[]{:S(2)}) %collective-permute-start.18) | collective-permute-done | bytes 524320 | tf_op jit(solution)/shard_map/ppermute | solution.py:407
  126.9 11.0 %collective-permute-done.24 = bf16[128,2048]{1,0:T(8,128)(2,1)S(1)} collective-permute-done((bf16[128,2048]{1,0:T(8,128)(2,1)S(1)}, bf16[128,2048]{1,0:T(8,128)(2,1)S(1)}, u32[]{:S(2)}, u32[]{:S(2)}) %collective-permute-start.24) | collective-permute-done | bytes 524320 | tf_op jit(solution)/shard_map/ppermute | solution.py:407
  137.9 2.2 add_convert_fusion.3
  140.1 4.4 %collective-permute-start.19 = (bf16[128,2048]{1,0:T(8,128)(2,1)S(1)}, bf16[128,2048]{1,0:T(8,128)(2,1)S(1)}, u32[]{:S(2)}, u32[]{:S(2)}) collective-permute-start(bf16[128,2048]{1,0:T(8,128)(2,1)S(1)} %get-tuple-element.27), channel_id=1, source_target_pairs={{0,1},{1,2},{4,5},{5,6},{8,9},{9,10},{12,13},{13,14},{16,17},{17,1... | collective-permute-start | bytes 1572872 | tf_op jit(solution)/shard_map/ppermute | solution.py:407
  144.5 4.9 %collective-permute-start.25 = (bf16[128,2048]{1,0:T(8,128)(2,1)S(1)}, bf16[128,2048]{1,0:T(8,128)(2,1)S(1)}, u32[]{:S(2)}, u32[]{:S(2)}) collective-permute-start(bf16[128,2048]{1,0:T(8,128)(2,1)S(1)} %get-tuple-element.30), channel_id=1, source_target_pairs={{0,1},{1,2},{4,5},{5,6},{8,9},{9,10},{12,13},{13,14},{16,17},{17,1... | collective-permute-start | bytes 1572872 | tf_op jit(solution)/shard_map/ppermute | solution.py:407
  149.4 6.9 %project.5 = f32[256,2048]{1,0:T(8,128)} custom-call(s32[1]{0:T(128)} %bitcast.which, bf16[256,2048]{1,0:T(8,128)(2,1)} %bitcast.40, bf16[2048,8192]{1,0:T(8,128)(2,1)} %weight.9), custom_call_target="tpu_custom_call" | custom-call | flops 2147483648 | bytes 10485760 | tf_op jit(solution)/shard_map/project/pallas_call | solution.py:320
  156.3 6.8 %project.6 = f32[256,2048]{1,0:T(8,128)} custom-call(s32[1]{0:T(128)} %bitcast.5.which, bf16[256,2048]{1,0:T(8,128)(2,1)} %bitcast.41, bf16[2048,8192]{1,0:T(8,128)(2,1)} %weight.9), custom_call_target="tpu_custom_call" | custom-call | flops 2147483648 | bytes 10485760 | tf_op jit(solution)/shard_map/project/pallas_call | solution.py:320
  163.1 7.0 %project.9 = f32[256,2048]{1,0:T(8,128)} custom-call(s32[1]{0:T(128)} %bitcast.8.which, bf16[256,2048]{1,0:T(8,128)(2,1)} %bitcast.42, bf16[2048,8192]{1,0:T(8,128)(2,1)} %weight.9), custom_call_target="tpu_custom_call" | custom-call | flops 2147483648 | bytes 10485760 | tf_op jit(solution)/shard_map/project/pallas_call | solution.py:320
  172.9 3.9 %collective-permute-start.20 = (bf16[128,2048]{1,0:T(8,128)(2,1)}, bf16[128,2048]{1,0:T(8,128)(2,1)}, u32[]{:S(2)}, u32[]{:S(2)}) collective-permute-start(bf16[128,2048]{1,0:T(8,128)(2,1)} %get-tuple-element.25), channel_id=1, source_target_pairs={{0,1},{1,2},{2,3},{4,5},{5,6},{6,7},{8,9},{9,10},{10,11},{12,13},{... | collective-permute-start | bytes 1572872 | tf_op jit(solution)/shard_map/ppermute | solution.py:407
  176.8 5.5 %collective-permute-start.26 = (bf16[128,2048]{1,0:T(8,128)(2,1)}, bf16[128,2048]{1,0:T(8,128)(2,1)}, u32[]{:S(2)}, u32[]{:S(2)}) collective-permute-start(bf16[128,2048]{1,0:T(8,128)(2,1)} %get-tuple-element.26), channel_id=1, source_target_pairs={{0,1},{1,2},{2,3},{4,5},{5,6},{6,7},{8,9},{9,10},{10,11},{12,13},{... | collective-permute-start | bytes 1572872 | tf_op jit(solution)/shard_map/ppermute | solution.py:407
  187.7 2.5 %gather_fusion = bf16[24,32,8,256]{3,2,1,0:T(8,128)(2,1)} fusion(bf16[8,32,8,256]{3,2,1,0:T(8,128)(2,1)S(1)} %bitcast.43, s32[1024]{0:T(1024)S(1)} %pad_clamp_fusion), kind=kCustom, calls=%fused_computation | custom fusion | bytes 6291552 | tf_op jit(solution)/shard_map/jit(_take)/gather | solution.py:426
  190.3 7.9 %collective-permute-done.26 = bf16[128,2048]{1,0:T(8,128)(2,1)} collective-permute-done((bf16[128,2048]{1,0:T(8,128)(2,1)}, bf16[128,2048]{1,0:T(8,128)(2,1)}, u32[]{:S(2)}, u32[]{:S(2)}) %collective-permute-start.26) | collective-permute-done | bytes 524320 | tf_op jit(solution)/shard_map/ppermute | solution.py:407
  198.2 14.5 %collective-permute-done.23 = bf16[128,2048]{1,0:T(8,128)(2,1)} collective-permute-done((bf16[128,2048]{1,0:T(8,128)(2,1)}, bf16[128,2048]{1,0:T(8,128)(2,1)}, u32[]{:S(2)}, u32[]{:S(2)}) %collective-permute-start.23) | collective-permute-done | bytes 524320 | tf_op jit(solution)/shard_map/ppermute | solution.py:407
  212.7 9.0 %collective-permute-done.29 = bf16[128,2048]{1,0:T(8,128)(2,1)} collective-permute-done((bf16[128,2048]{1,0:T(8,128)(2,1)}, bf16[128,2048]{1,0:T(8,128)(2,1)}, u32[]{:S(2)}, u32[]{:S(2)}) %collective-permute-start.29) | collective-permute-done | bytes 524320 | tf_op jit(solution)/shard_map/ppermute | solution.py:407
  221.7 2.1 fusion.13
  224.3 1.8 collective-permute-start.30
  226.1 2.4 %collective-permute-start.32 = (f32[2,128]{1,0:T(2,128)S(1)}, f32[2,128]{1,0:T(2,128)S(1)}, u32[]{:S(2)}, u32[]{:S(2)}) collective-permute-start(f32[2,128]{1,0:T(2,128)S(1)} %fusion), channel_id=1, source_target_pairs={{0,3},{1,0},{2,1},{3,2},{4,7},{5,4},{6,5},{7,6},{8,11},{9,8},{10,9... | collective-permute-start | bytes 3080 | tf_op jit(solution)/shard_map/ppermute | solution.py:445
  228.5 2.1 select_select_fusion
  (111 shorter events, 22.8 us)
Async XLA Ops:
  7.2 179.3 %all-gather.3.cloned.1.call-start = ((), (), s32[]{:S(2)}) async-start(), calls=%async_computation | async-start | bytes 1310720 | tf_op jit(solution)/shard_map/all_gather | solution.py:418
  13.2 10.3 %collective-permute-start.16 = (bf16[2,2,128,256]{3,2,1,0:T(8,128)(2,1)}, bf16[2,2,128,256]{3,2,1,0:T(8,128)(2,1)S(1)}, u32[]{:S(2)}, u32[]{:S(2)}) collective-permute-start(bf16[2,2,128,256]{3,2,1,0:T(8,128)(2,1)} %get-tuple-element.17.refs_12_), channel_id=1, source_target_pairs={{0,8},{4,12},{8,0},{12,4},{1,9},{5,13},{9,1},{13,5},{2,10},{6,14},... | collective-permute-start | bytes 786440 | tf_op jit(solution)/shard_map/ppermute | solution.py:347
  16.2 14.1 %collective-permute-start.7 = (bf16[12,2,32,256]{3,2,1,0:T(8,128)(2,1)}, bf16[12,2,32,256]{3,2,1,0:T(8,128)(2,1)S(1)}, u32[]{:S(2)}, u32[]{:S(2)}) collective-permute-start(bf16[12,2,32,256]{3,2,1,0:T(8,128)(2,1)} %get-tuple-element.15), channel_id=1, source_target_pairs={{0,1},{1,2},{2,3},{3,0},{4,5},{5,6},{6,7},{7,4},{8,9},{9,10},{10,1... | collective-permute-start | bytes 1179656 | tf_op jit(solution)/shard_map/ppermute | solution.py:374
  17.8 18.9 %collective-permute-start.11 = (bf16[12,2,32,256]{3,2,1,0:T(8,128)(2,1)}, bf16[12,2,32,256]{3,2,1,0:T(8,128)(2,1)S(1)}, u32[]{:S(2)}, u32[]{:S(2)}) collective-permute-start(bf16[12,2,32,256]{3,2,1,0:T(8,128)(2,1)} %get-tuple-element.16), channel_id=1, source_target_pairs={{0,3},{1,0},{2,1},{3,2},{4,7},{5,4},{6,5},{7,6},{8,11},{9,8},{10,9... | collective-permute-start | bytes 1179656 | tf_op jit(solution)/shard_map/ppermute | solution.py:374
  20.1 17.2 %collective-permute-start.5 = (bf16[12,2,32,256]{3,2,1,0:T(8,128)(2,1)}, bf16[12,2,32,256]{3,2,1,0:T(8,128)(2,1)S(1)}, u32[]{:S(2)}, u32[]{:S(2)}) collective-permute-start(bf16[12,2,32,256]{3,2,1,0:T(8,128)(2,1)} %get-tuple-element.14.refs_0_), channel_id=1, source_target_pairs={{0,8},{4,12},{8,0},{12,4},{1,9},{5,13},{9,1},{13,5},{2,10},{6,14},... | collective-permute-start | bytes 1179656 | tf_op jit(solution)/shard_map/ppermute | solution.py:347
  23.5 13.8 %collective-permute-start.4 = (bf16[12,2,32,256]{3,2,1,0:T(8,128)(2,1)}, bf16[12,2,32,256]{3,2,1,0:T(8,128)(2,1)S(1)}, u32[]{:S(2)}, u32[]{:S(2)}) collective-permute-start(bf16[12,2,32,256]{3,2,1,0:T(8,128)(2,1)} %get-tuple-element.14.refs_0_), channel_id=1, source_target_pairs={{0,4},{4,0},{8,12},{12,8},{1,5},{5,1},{9,13},{13,9},{2,6},{6,2},{1... | collective-permute-start | bytes 1179656 | tf_op jit(solution)/shard_map/ppermute | solution.py:348
  23.5 30.6 %collective-permute-start = (bf16[12,2,32,256]{3,2,1,0:T(8,128)(2,1)}, bf16[12,2,32,256]{3,2,1,0:T(8,128)(2,1)S(1)}, u32[]{:S(2)}, u32[]{:S(2)}) collective-permute-start(bf16[12,2,32,256]{3,2,1,0:T(8,128)(2,1)} %get-tuple-element.13), channel_id=1, source_target_pairs={{0,2},{1,3},{2,0},{3,1},{4,6},{5,7},{6,4},{7,5},{8,10},{9,11},{10,... | collective-permute-start | bytes 1179656 | tf_op jit(solution)/shard_map/ppermute | solution.py:374
  30.3 24.4 %collective-permute-start.9 = (bf16[12,2,32,256]{3,2,1,0:T(8,128)(2,1)S(1)}, bf16[12,2,32,256]{3,2,1,0:T(8,128)(2,1)S(1)}, u32[]{:S(2)}, u32[]{:S(2)}) collective-permute-start(bf16[12,2,32,256]{3,2,1,0:T(8,128)(2,1)S(1)} %collective-permute-done.7.refs_4_), channel_id=1, source_target_pairs={{0,8},{4,12},{8,0},{12,4},{1,9},{5,13},{9,1},{13,5},{2,10},{6,14},... | collective-permute-start | bytes 1179656 | tf_op jit(solution)/shard_map/ppermute | solution.py:347
  36.7 18.5 %collective-permute-start.13 = (bf16[12,2,32,256]{3,2,1,0:T(8,128)(2,1)S(1)}, bf16[12,2,32,256]{3,2,1,0:T(8,128)(2,1)S(1)}, u32[]{:S(2)}, u32[]{:S(2)}) collective-permute-start(bf16[12,2,32,256]{3,2,1,0:T(8,128)(2,1)S(1)} %collective-permute-done.11.refs_8_), channel_id=1, source_target_pairs={{0,8},{4,12},{8,0},{12,4},{1,9},{5,13},{9,1},{13,5},{2,10},{6,14},... | collective-permute-start | bytes 1179656 | tf_op jit(solution)/shard_map/ppermute | solution.py:347
  37.3 18.0 %collective-permute-start.6 = (bf16[12,2,32,256]{3,2,1,0:T(8,128)(2,1)S(1)}, bf16[12,2,32,256]{3,2,1,0:T(8,128)(2,1)S(1)}, u32[]{:S(2)}, u32[]{:S(2)}) collective-permute-start(bf16[12,2,32,256]{3,2,1,0:T(8,128)(2,1)S(1)} %collective-permute-done.5.refs_2_), channel_id=1, source_target_pairs={{0,4},{4,0},{8,12},{12,8},{1,5},{5,1},{9,13},{13,9},{2,6},{6,2},{1... | collective-permute-start | bytes 1179656 | tf_op jit(solution)/shard_map/ppermute | solution.py:348
  37.3 16.9 %collective-permute-start.17 = (bf16[2,2,128,256]{3,2,1,0:T(8,128)(2,1)S(1)}, bf16[2,2,128,256]{3,2,1,0:T(8,128)(2,1)}, u32[]{:S(2)}, u32[]{:S(2)}) collective-permute-start(bf16[2,2,128,256]{3,2,1,0:T(8,128)(2,1)S(1)} %collective-permute-done.16.refs_14_), channel_id=1, source_target_pairs={{0,4},{4,0},{8,12},{12,8},{1,5},{5,1},{9,13},{13,9},{2,6},{6,2},{1... | collective-permute-start | bytes 786440 | tf_op jit(solution)/shard_map/ppermute | solution.py:348
  54.2 17.1 %collective-permute-start.8 = (bf16[12,2,32,256]{3,2,1,0:T(8,128)(2,1)S(1)}, bf16[12,2,32,256]{3,2,1,0:T(8,128)(2,1)}, u32[]{:S(2)}, u32[]{:S(2)}) collective-permute-start(bf16[12,2,32,256]{3,2,1,0:T(8,128)(2,1)S(1)} %collective-permute-done.7.refs_4_), channel_id=1, source_target_pairs={{0,4},{4,0},{8,12},{12,8},{1,5},{5,1},{9,13},{13,9},{2,6},{6,2},{1... | collective-permute-start | bytes 1179656 | tf_op jit(solution)/shard_map/ppermute | solution.py:348
  54.7 16.6 %collective-permute-start.2 = (bf16[12,2,32,256]{3,2,1,0:T(8,128)(2,1)S(1)}, bf16[12,2,32,256]{3,2,1,0:T(8,128)(2,1)S(1)}, u32[]{:S(2)}, u32[]{:S(2)}) collective-permute-start(bf16[12,2,32,256]{3,2,1,0:T(8,128)(2,1)S(1)} %collective-permute-done.refs_0_), channel_id=1, source_target_pairs={{0,8},{4,12},{8,0},{12,4},{1,9},{5,13},{9,1},{13,5},{2,10},{6,14},... | collective-permute-start | bytes 1179656 | tf_op jit(solution)/shard_map/ppermute | solution.py:347
  55.3 16.0 %collective-permute-start.10 = (bf16[12,2,32,256]{3,2,1,0:T(8,128)(2,1)S(1)}, bf16[12,2,32,256]{3,2,1,0:T(8,128)(2,1)}, u32[]{:S(2)}, u32[]{:S(2)}) collective-permute-start(bf16[12,2,32,256]{3,2,1,0:T(8,128)(2,1)S(1)} %collective-permute-done.9.refs_6_), channel_id=1, source_target_pairs={{0,4},{4,0},{8,12},{12,8},{1,5},{5,1},{9,13},{13,9},{2,6},{6,2},{1... | collective-permute-start | bytes 1179656 | tf_op jit(solution)/shard_map/ppermute | solution.py:348
  55.3 16.0 %collective-permute-start.14 = (bf16[12,2,32,256]{3,2,1,0:T(8,128)(2,1)S(1)}, bf16[12,2,32,256]{3,2,1,0:T(8,128)(2,1)}, u32[]{:S(2)}, u32[]{:S(2)}) collective-permute-start(bf16[12,2,32,256]{3,2,1,0:T(8,128)(2,1)S(1)} %collective-permute-done.13.refs_10_), channel_id=1, source_target_pairs={{0,4},{4,0},{8,12},{12,8},{1,5},{5,1},{9,13},{13,9},{2,6},{6,2},{1... | collective-permute-start | bytes 1179656 | tf_op jit(solution)/shard_map/ppermute | solution.py:348
  56.3 38.3 %collective-permute-start.1 = (bf16[12,2,32,256]{3,2,1,0:T(8,128)(2,1)S(1)}, bf16[12,2,32,256]{3,2,1,0:T(8,128)(2,1)S(1)}, u32[]{:S(2)}, u32[]{:S(2)}) collective-permute-start(bf16[12,2,32,256]{3,2,1,0:T(8,128)(2,1)S(1)} %collective-permute-done.refs_0_), channel_id=1, source_target_pairs={{0,4},{4,0},{8,12},{12,8},{1,5},{5,1},{9,13},{13,9},{2,6},{6,2},{1... | collective-permute-start | bytes 1179656 | tf_op jit(solution)/shard_map/ppermute | solution.py:348
  71.3 23.4 %collective-permute-start.3 = (bf16[12,2,32,256]{3,2,1,0:T(8,128)(2,1)S(1)}, bf16[12,2,32,256]{3,2,1,0:T(8,128)(2,1)S(1)}, u32[]{:S(2)}, u32[]{:S(2)}) collective-permute-start(bf16[12,2,32,256]{3,2,1,0:T(8,128)(2,1)S(1)} %collective-permute-done.2.refs_2_), channel_id=1, source_target_pairs={{0,4},{4,0},{8,12},{12,8},{1,5},{5,1},{9,13},{13,9},{2,6},{6,2},{1... | collective-permute-start | bytes 1179656 | tf_op jit(solution)/shard_map/ppermute | solution.py:348
  113.3 13.6 %collective-permute-start.18 = (bf16[128,2048]{1,0:T(8,128)(2,1)S(1)}, bf16[128,2048]{1,0:T(8,128)(2,1)S(1)}, u32[]{:S(2)}, u32[]{:S(2)}) collective-permute-start(bf16[128,2048]{1,0:T(8,128)(2,1)S(1)} %get-tuple-element.33), channel_id=1, source_target_pairs={{0,1},{4,5},{8,9},{12,13},{16,17},{20,21},{24,25},{28,29}} | collective-permute-start | bytes 1572872 | tf_op jit(solution)/shard_map/ppermute | solution.py:407
  114.6 12.3 %collective-permute-start.21 = (bf16[128,2048]{1,0:T(8,128)(2,1)S(1)}, bf16[128,2048]{1,0:T(8,128)(2,1)S(1)}, u32[]{:S(2)}, u32[]{:S(2)}) collective-permute-start(bf16[128,2048]{1,0:T(8,128)(2,1)S(1)} %get-tuple-element.33), channel_id=1, source_target_pairs={{3,2},{7,6},{11,10},{15,14},{19,18},{23,22},{27,26},{31,30}} | collective-permute-start | bytes 1572872 | tf_op jit(solution)/shard_map/ppermute | solution.py:407
  115.3 22.5 %collective-permute-start.24 = (bf16[128,2048]{1,0:T(8,128)(2,1)S(1)}, bf16[128,2048]{1,0:T(8,128)(2,1)S(1)}, u32[]{:S(2)}, u32[]{:S(2)}) collective-permute-start(bf16[128,2048]{1,0:T(8,128)(2,1)S(1)} %get-tuple-element.34), channel_id=1, source_target_pairs={{0,1},{4,5},{8,9},{12,13},{16,17},{20,21},{24,25},{28,29}} | collective-permute-start | bytes 1572872 | tf_op jit(solution)/shard_map/ppermute | solution.py:407
  116.7 21.2 %collective-permute-start.27 = (bf16[128,2048]{1,0:T(8,128)(2,1)S(1)}, bf16[128,2048]{1,0:T(8,128)(2,1)S(1)}, u32[]{:S(2)}, u32[]{:S(2)}) collective-permute-start(bf16[128,2048]{1,0:T(8,128)(2,1)S(1)} %get-tuple-element.34), channel_id=1, source_target_pairs={{3,2},{7,6},{11,10},{15,14},{19,18},{23,22},{27,26},{31,30}} | collective-permute-start | bytes 1572872 | tf_op jit(solution)/shard_map/ppermute | solution.py:407
  140.1 31.5 %collective-permute-start.19 = (bf16[128,2048]{1,0:T(8,128)(2,1)S(1)}, bf16[128,2048]{1,0:T(8,128)(2,1)S(1)}, u32[]{:S(2)}, u32[]{:S(2)}) collective-permute-start(bf16[128,2048]{1,0:T(8,128)(2,1)S(1)} %get-tuple-element.27), channel_id=1, source_target_pairs={{0,1},{1,2},{4,5},{5,6},{8,9},{9,10},{12,13},{13,14},{16,17},{17,1... | collective-permute-start | bytes 1572872 | tf_op jit(solution)/shard_map/ppermute | solution.py:407
  144.5 27.1 %collective-permute-start.25 = (bf16[128,2048]{1,0:T(8,128)(2,1)S(1)}, bf16[128,2048]{1,0:T(8,128)(2,1)S(1)}, u32[]{:S(2)}, u32[]{:S(2)}) collective-permute-start(bf16[128,2048]{1,0:T(8,128)(2,1)S(1)} %get-tuple-element.30), channel_id=1, source_target_pairs={{0,1},{1,2},{4,5},{5,6},{8,9},{9,10},{12,13},{13,14},{16,17},{17,1... | collective-permute-start | bytes 1572872 | tf_op jit(solution)/shard_map/ppermute | solution.py:407
  170.1 12.2 %collective-permute-start.22 = (bf16[128,2048]{1,0:T(8,128)(2,1)S(1)}, bf16[128,2048]{1,0:T(8,128)(2,1)S(1)}, u32[]{:S(2)}, u32[]{:S(2)}) collective-permute-start(bf16[128,2048]{1,0:T(8,128)(2,1)S(1)} %get-tuple-element.28), channel_id=1, source_target_pairs={{2,1},{3,2},{6,5},{7,6},{10,9},{11,10},{14,13},{15,14},{18,17},{19... | collective-permute-start | bytes 1572872 | tf_op jit(solution)/shard_map/ppermute | solution.py:407
  170.8 11.5 %collective-permute-start.28 = (bf16[128,2048]{1,0:T(8,128)(2,1)S(1)}, bf16[128,2048]{1,0:T(8,128)(2,1)S(1)}, u32[]{:S(2)}, u32[]{:S(2)}) collective-permute-start(bf16[128,2048]{1,0:T(8,128)(2,1)S(1)} %get-tuple-element.29), channel_id=1, source_target_pairs={{2,1},{3,2},{6,5},{7,6},{10,9},{11,10},{14,13},{15,14},{18,17},{19... | collective-permute-start | bytes 1572872 | tf_op jit(solution)/shard_map/ppermute | solution.py:407
  172.9 17.4 %collective-permute-start.20 = (bf16[128,2048]{1,0:T(8,128)(2,1)}, bf16[128,2048]{1,0:T(8,128)(2,1)}, u32[]{:S(2)}, u32[]{:S(2)}) collective-permute-start(bf16[128,2048]{1,0:T(8,128)(2,1)} %get-tuple-element.25), channel_id=1, source_target_pairs={{0,1},{1,2},{2,3},{4,5},{5,6},{6,7},{8,9},{9,10},{10,11},{12,13},{... | collective-permute-start | bytes 1572872 | tf_op jit(solution)/shard_map/ppermute | solution.py:407
  176.8 21.5 %collective-permute-start.26 = (bf16[128,2048]{1,0:T(8,128)(2,1)}, bf16[128,2048]{1,0:T(8,128)(2,1)}, u32[]{:S(2)}, u32[]{:S(2)}) collective-permute-start(bf16[128,2048]{1,0:T(8,128)(2,1)} %get-tuple-element.26), channel_id=1, source_target_pairs={{0,1},{1,2},{2,3},{4,5},{5,6},{6,7},{8,9},{9,10},{10,11},{12,13},{... | collective-permute-start | bytes 1572872 | tf_op jit(solution)/shard_map/ppermute | solution.py:407
  183.5 29.2 %collective-permute-start.23 = (bf16[128,2048]{1,0:T(8,128)(2,1)}, bf16[128,2048]{1,0:T(8,128)(2,1)}, u32[]{:S(2)}, u32[]{:S(2)}) collective-permute-start(bf16[128,2048]{1,0:T(8,128)(2,1)} %get-tuple-element.31), channel_id=1, source_target_pairs={{1,0},{2,1},{3,2},{5,4},{6,5},{7,6},{9,8},{10,9},{11,10},{13,12},{... | collective-permute-start | bytes 1572872 | tf_op jit(solution)/shard_map/ppermute | solution.py:407
  184.8 36.9 %collective-permute-start.29 = (bf16[128,2048]{1,0:T(8,128)(2,1)}, bf16[128,2048]{1,0:T(8,128)(2,1)}, u32[]{:S(2)}, u32[]{:S(2)}) collective-permute-start(bf16[128,2048]{1,0:T(8,128)(2,1)} %get-tuple-element.32), channel_id=1, source_target_pairs={{1,0},{2,1},{3,2},{5,4},{6,5},{7,6},{9,8},{10,9},{11,10},{13,12},{... | collective-permute-start | bytes 1572872 | tf_op jit(solution)/shard_map/ppermute | solution.py:407
  224.3 6.3 %collective-permute-start.30 = (f32[2,128]{1,0:T(2,128)S(1)}, f32[2,128]{1,0:T(2,128)S(1)}, u32[]{:S(2)}, u32[]{:S(2)}) collective-permute-start(f32[2,128]{1,0:T(2,128)S(1)} %fusion), channel_id=1, source_target_pairs={{0,1},{1,2},{2,3},{3,0},{4,5},{5,6},{6,7},{7,4},{8,9},{9,10},{10,1... | collective-permute-start | bytes 3080 | tf_op jit(solution)/shard_map/ppermute | solution.py:445
  226.0 4.5 %collective-permute-start.31 = (f32[2,128]{1,0:T(2,128)S(1)}, f32[2,128]{1,0:T(2,128)S(1)}, u32[]{:S(2)}, u32[]{:S(2)}) collective-permute-start(f32[2,128]{1,0:T(2,128)S(1)} %fusion), channel_id=1, source_target_pairs={{0,2},{1,3},{2,0},{3,1},{4,6},{5,7},{6,4},{7,5},{8,10},{9,11},{10,... | collective-permute-start | bytes 3080 | tf_op jit(solution)/shard_map/ppermute | solution.py:445
  226.1 4.5 %collective-permute-start.32 = (f32[2,128]{1,0:T(2,128)S(1)}, f32[2,128]{1,0:T(2,128)S(1)}, u32[]{:S(2)}, u32[]{:S(2)}) collective-permute-start(f32[2,128]{1,0:T(2,128)S(1)} %fusion), channel_id=1, source_target_pairs={{0,3},{1,0},{2,1},{3,2},{4,7},{5,4},{6,5},{7,6},{8,11},{9,8},{10,9... | collective-permute-start | bytes 3080 | tf_op jit(solution)/shard_map/ppermute | solution.py:445
  (24 other events, 446.4 us)
Sparse Core Ops, SparseCore 0:
  39.7 30.0 all-gather.2

commit v2 on v1

v2 whole, which is shorter than its diff:
```python
import functools
import math

import jax
import jax.numpy as jnp
from jax import lax
from jax.experimental import pallas as pl
from jax.experimental.pallas import tpu as pltpu
from jax.sharding import PartitionSpec as P

QH = 64
KVH = 8
HD = 128
MAXB = 24
MOST = 12

epsilon = 1e-05
lowest = -1e30
exponent_scale = math.log2(math.e) / math.sqrt(HD)
VMEM_LIMIT = 56 * 1024 * 1024
WEIGHT_PARTS = 4
TILE_CHUNKS = 2

SMEM = functools.partial(pl.BlockSpec, memory_space=pltpu.SMEM)
VMEM = functools.partial(pl.BlockSpec, memory_space=pltpu.VMEM)
ANY = functools.partial(pl.BlockSpec, memory_space=pl.ANY)


def holder_of(relative, pool_index, pool_count):
    chips = pool_count // 2
    chip = lax.rem(pool_index // 2 + chips - relative // 2, chips)
    core = lax.rem(lax.rem(pool_index, 2) + relative % 2, 2)
    return chip * 2 + core


def spread(block, wide):
    rows = block.shape[0]
    for half in range(2):
        wide[half, pl.ds(0, rows * KVH), :] = (
            block[:, :, half * HD : (half + 1) * HD].astype(jnp.float32).reshape(rows * KVH, HD)
        )


def one_head(head, rows, wide):
    here = pl.ds(head, rows, stride=KVH)
    return jnp.concatenate([wide[half, here, :] for half in range(2)], axis=1).astype(jnp.bfloat16)


def first_head(device, heads_dev):
    return device * heads_dev // (QH // KVH)


def prepare_kernel(tp_count, pool_count, heads_dev, hit, lens, place, pool, *refs):
    counts, needed = refs[:2]
    sends = refs[2 : 2 + tp_count]
    own_slots, held, wide, sems = refs[2 + tp_count :]
    prompts = counts.shape[0]
    slots_dev, block_rows = pool.shape[:2]
    kv_dev = sends[0].shape[1]
    pool_index = place[0]
    tp_index = place[1]
    for slot in range(MOST + 1):
        own_slots[slot] = 0
    for prompt in range(prompts):
        for relative in range(pool_count):
            counts[prompt, relative] = 0

        def entry(position, carry, prompt=prompt):
            block = hit[prompt, position]
            holder = block // slots_dev
            chips = pool_count // 2
            chip_away = lax.rem(pool_index // 2 + chips - holder // 2, chips)
            core_away = lax.rem(lax.rem(pool_index, 2) + lax.rem(holder, 2), 2)
            relative = chip_away * 2 + core_away
            counts[prompt, relative] = counts[prompt, relative] + 1

            @pl.when(holder == pool_index)
            def _():
                rank = own_slots[MOST]
                own_slots[rank] = block - holder * slots_dev
                own_slots[MOST] = rank + 1

            return carry

        lax.fori_loop(0, lens[prompt], entry, 0)
    copies = []
    for slot in range(MOST):
        copy = pltpu.make_async_copy(pool.at[own_slots[slot]], held.at[slot], sems.at[slot])
        copy.start()
        copies.append(copy)
    for at in range(tp_count):
        away = jnp.where(tp_index < tp_count // 2, -1 - at, 1 + at)
        needed[at] = lax.rem(tp_index + away + 2 * tp_count, tp_count)
    for slot in range(MOST):
        copies[slot].wait()
        spread(held[slot], wide)
        for shift in range(tp_count):
            head = first_head(lax.rem(tp_index + shift, tp_count), heads_dev)
            for more in range(kv_dev):
                sends[shift][slot, more] = one_head(head + more, block_rows, wide)


def prepare(tp_count, pool_count, heads_dev, kv_dev, hit, lens, place, pool):
    prompts = lens.shape[0]
    block_rows = pool.shape[1]
    send = jax.ShapeDtypeStruct((MOST, kv_dev, block_rows, 2 * HD), jnp.bfloat16)
    counts, needed, *sends = pl.pallas_call(
        functools.partial(prepare_kernel, tp_count, pool_count, heads_dev),
        out_shape=[
            jax.ShapeDtypeStruct((prompts, pool_count), jnp.int32),
            jax.ShapeDtypeStruct((tp_count,), jnp.int32),
        ]
        + [send] * tp_count,
        in_specs=[SMEM(), SMEM(), SMEM(), ANY()],
        out_specs=[SMEM()] * 2 + [VMEM()] * tp_count,
        scratch_shapes=[
            pltpu.SMEM((MOST + 1,), jnp.int32),
            pltpu.VMEM((MOST, block_rows, KVH, 2 * HD), jnp.bfloat16),
            pltpu.VMEM((2, block_rows * KVH, HD), jnp.float32),
            pltpu.SemaphoreType.DMA((MOST,)),
        ],
        compiler_params=pltpu.CompilerParams(vmem_limit_bytes=VMEM_LIMIT),
        cost_estimate=pl.CostEstimate(flops=0, bytes_accessed=8 << 20, transcendentals=0),
        name="prepare",
    )(hit, lens, place, pool)
    return counts, needed, sends


def span_kernel(heads_dev, place, span, heads, pieces, wide):
    prompts, rows_dev = span.shape[:2]
    block_rows = pieces.shape[1]
    tp_index = place[1]
    for prompt in range(prompts):
        here = pl.ds(pl.multiple_of(tp_index * block_rows, block_rows), block_rows)
        pieces[prompt] = span[prompt, here]
        spread(span[prompt], wide)
        for more in range(heads.shape[0]):
            heads[more, prompt] = one_head(first_head(tp_index, heads_dev) + more, rows_dev, wide)


def span_parts(heads_dev, kv_dev, block_rows, place, span):
    prompts, rows_dev = span.shape[:2]
    return pl.pallas_call(
        functools.partial(span_kernel, heads_dev),
        out_shape=[
            jax.ShapeDtypeStruct((kv_dev, prompts, rows_dev, 2 * HD), jnp.bfloat16),
            jax.ShapeDtypeStruct((prompts, block_rows, KVH, 2 * HD), jnp.bfloat16),
        ],
        in_specs=[SMEM(), VMEM()],
        out_specs=[VMEM()] * 2,
        scratch_shapes=[pltpu.VMEM((2, rows_dev * KVH, HD), jnp.float32)],
        compiler_params=pltpu.CompilerParams(vmem_limit_bytes=VMEM_LIMIT),
        cost_estimate=pl.CostEstimate(flops=0, bytes_accessed=2 << 20, transcendentals=0),
        name="span_parts",
    )(place, span)


def attend_kernel(
    which_prompts, n_chunks, pool_count, kv_dev, pieces, with_span, with_state, final, block_heads, *refs
):
    refs = list(refs)
    place, lens, counts, query = [refs.pop(0) for _ in range(4)]
    chunk_refs = [
        [[refs.pop(0) for _ in range(pool_count)] for _ in range(pieces[chunk])]
        for chunk in range(n_chunks)
    ]
    span_refs = [refs.pop(0) for _ in range(pool_count)] if with_span else []
    state_in = refs.pop(0) if with_state else None
    which, out_w = [refs.pop(0) for _ in range(2)] if final else (None, None)
    prompts = len(which_prompts)
    if final:
        attended = [refs.pop(0) for _ in range(prompts)]
        projected = [refs.pop(0) for _ in range(prompts)]
    else:
        state_out = refs.pop(0)
    asked_all, blocks, keys, valued, sems = [refs.pop(0) for _ in range(5)]
    span_blocks, span_keys, span_valued = [refs.pop(0) for _ in range(3)] if with_span else [None] * 3
    state = refs.pop(0) if with_state else None
    weight = refs.pop(0) if final else None
    pool_index = place[0]
    rows_dev = asked_all.shape[1]
    block_rows = blocks.shape[3]
    key_rows = MAXB * block_rows
    group = asked_all.shape[2] // HD // kv_dev
    held = keys.dtype
    rows = block_heads * rows_dev

    started = []

    def start(source, target):
        copy = pltpu.make_async_copy(source, target, sems.at[len(started)])
        copy.start()
        started.append(copy)
        return copy

    brought = []
    for head in range(kv_dev):
        mine = []
        for at, prompt in enumerate(which_prompts):
            if head == 0:
                mine.append(start(query.at[prompt], asked_all.at[at]))
            if with_span:
                mine += [
                    start(span_refs[r].at[head, prompt], span_blocks.at[head, r, at])
                    for r in range(pool_count)
                ]
        for chunk in range(n_chunks):
            split = pieces[chunk] > 1
            for r in range(pool_count):
                source = chunk_refs[chunk][head if split else 0][r]
                mine.append(
                    start(
                        source.at[:, 0 if split else head], blocks.at[head, chunk * pool_count + r]
                    )
                )
        if with_state:
            mine.append(start(state_in.at[head], state.at[head]))
        brought.append(mine)
    late = []
    if final:
        width = weight.shape[1]
        part = weight.shape[0] // WEIGHT_PARTS
        columns = pl.ds(pl.multiple_of(which[0] * width, width), width)
    if with_span:
        place_in = lax.broadcasted_iota(jnp.int32, (1, rows_dev), 1)
        key_pos = jnp.concatenate(
            [holder_of(r, pool_index, pool_count) * rows_dev + place_in for r in range(pool_count)],
            axis=1,
        )
        query_pos = pool_index * rows_dev + lax.rem(
            lax.broadcasted_iota(jnp.int32, (rows, 1), 0), rows_dev
        )

    def gather(head, prompt):
        for chunk in range(n_chunks):
            offset = jnp.int32(0)
            for r in range(pool_count):
                first = jnp.int32(0)
                for other in range(which_prompts[prompt]):
                    first += counts[other, r]

                def bring(index, carry, at=chunk * pool_count + r, first=first, offset=offset):
                    block = blocks[head, at, first + index].astype(held)
                    here = pl.ds(
                        pl.multiple_of((offset + index) * block_rows, block_rows), block_rows
                    )
                    keys[head, prompt, chunk, here, :] = block[:, :HD]
                    valued[head, prompt, chunk, here, :HD] = block[:, HD:]
                    valued[head, prompt, chunk, here, HD:] = jnp.ones((block_rows, HD), held)
                    return carry

                count = counts[which_prompts[prompt], r]
                lax.fori_loop(0, count, bring, 0)
                offset += count

            def fill(index, carry):
                here = pl.ds(pl.multiple_of(index * block_rows, block_rows), block_rows)
                keys[head, prompt, chunk, here, :] = keys[
                    head, prompt, chunk, pl.ds(0, block_rows), :
                ]
                valued[head, prompt, chunk, here, :] = jnp.zeros((block_rows, 2 * HD), held)
                return carry

            lax.fori_loop(offset, MAXB, fill, 0)
        if with_span:
            for r in range(pool_count):
                here = pl.ds(r * rows_dev, rows_dev)
                block = span_blocks[head, r, prompt]
                span_keys[head, prompt, here, :] = block[:, :HD]
                span_valued[head, prompt, here, :HD] = block[:, HD:]
                span_valued[head, prompt, here, HD:] = jnp.ones((rows_dev, HD), jnp.bfloat16)

    def score(head, prompt, first, chunk):
        heads = range(head * group + first, head * group + first + block_heads)
        asked = jnp.concatenate(
            [asked_all[prompt, :, h * HD : (h + 1) * HD] for h in heads], axis=0
        )
        if chunk is None:
            key_part = span_keys[head, prompt]
        else:
            key_part = keys[head, prompt, chunk : chunk + TILE_CHUNKS].reshape(-1, HD)
        key_part = key_part.astype(jnp.bfloat16)
        scores = lax.dot_general(
            asked, key_part, (((1,), (1,)), ((), ())), preferred_element_type=jnp.float32
        )
        if chunk is None:
            return jnp.where(key_pos <= query_pos, scores, lowest)
        return scores

    tiles = ([None] if with_span else []) + list(range(0, n_chunks, TILE_CHUNKS))

    def score_of(head, prompt, first, at):
        return score(head, prompt, first, tiles[at])

    for head in range(kv_dev):
        for copy in brought[head]:
            copy.wait()
        if final and head == 0:
            late = [
                start(out_w.at[pl.ds(i * part, part), columns], weight.at[pl.ds(i * part, part)])
                for i in range(WEIGHT_PARTS)
            ]
        for prompt in range(prompts):
            gather(head, prompt)
        work = [
            (head, prompt, first, at)
            for prompt in range(prompts)
            for first in range(0, group, block_heads)
            for at in range(len(tiles))
        ]
        ahead = score_of(*work[0])
        for n, (_, prompt, first, at) in enumerate(work):
            scores = ahead
            if n + 1 < len(work):
                ahead = score_of(*work[n + 1])
            here = pl.ds(first * rows_dev, rows)
            running = None if at == 0 else running
            if at == 0 and with_state:
                before = state[head, prompt, here, :]
                running = [before[:, 2 * HD - 1 :], before]
            peak = jnp.max(scores, axis=1, keepdims=True)
            if running is not None:
                peak = jnp.maximum(running[0], peak)
            weights = jnp.exp2((scores - peak) * exponent_scale).astype(jnp.bfloat16)
            chunk = tiles[at]
            if chunk is None:
                value_part = span_valued[head, prompt]
            else:
                value_part = valued[head, prompt, chunk : chunk + TILE_CHUNKS].reshape(-1, 2 * HD)
            result = jnp.dot(
                weights, value_part.astype(jnp.bfloat16), preferred_element_type=jnp.float32
            )
            if running is not None:
                result += running[1] * jnp.exp2((running[0] - peak) * exponent_scale)
            running = [peak, result]
            if at < len(tiles) - 1:
                continue
            if not final:
                state_out[head, prompt, here, :HD] = result[:, :HD]
                lanes = lax.broadcasted_iota(jnp.int32, (rows, HD), 1)
                state_out[head, prompt, here, HD:] = jnp.where(lanes < HD // 2, result[:, HD:], peak)
                continue
            total = result[:, HD : HD + 1] if with_state else result[:, HD:]
            done = (result[:, :HD] / total).astype(jnp.bfloat16)
            for m in range(block_heads):
                h = head * group + first + m
                attended[prompt][:, h * HD : (h + 1) * HD] = done[m * rows_dev : (m + 1) * rows_dev]
    for copy in late:
        copy.wait()
    if final:
        together = jnp.concatenate([ref[...] for ref in attended], axis=0)
        tile = min(512, width)
        for at in range(0, width, tile):
            total = jnp.dot(
                together, weight[:, at : at + tile], preferred_element_type=jnp.float32
            ).astype(jnp.bfloat16)
            for prompt in range(prompts):
                projected[prompt][:, at : at + tile] = total[
                    prompt * rows_dev : (prompt + 1) * rows_dev
                ]


def attend(
    which_prompts, place, lens, counts, queries, chunks, kv_dev, span=None, state=None, out_w=None, which=None, width=0
):
    pool_count = len(chunks[0][0])
    n_chunks = len(chunks)
    prompts = len(which_prompts)
    rows_dev, features = queries.shape[1:]
    group = features // HD // kv_dev
    block_rows = chunks[0][0][0].shape[2]
    key_rows = MAXB * block_rows
    held = jnp.bfloat16 if block_rows % 16 == 0 else jnp.float32
    block_heads = min(8, group)
    final = out_w is not None
    state_shape = (kv_dev, prompts, group * rows_dev, 2 * HD)
    operands = [place, lens, counts, queries]
    operands += [array for chunk in chunks for piece in chunk for array in piece]
    copies = prompts + kv_dev * n_chunks * pool_count
    n_keys = key_rows * n_chunks
    scratch = [
        pltpu.VMEM((prompts, rows_dev, features), jnp.bfloat16),
        pltpu.VMEM((kv_dev, n_chunks * pool_count, MOST, block_rows, 2 * HD), jnp.bfloat16),
        pltpu.VMEM((kv_dev, prompts, n_chunks, key_rows, HD), held),
        pltpu.VMEM((kv_dev, prompts, n_chunks, key_rows, 2 * HD), held),
    ]
    later = []
    if span is not None:
        operands += span
        copies += prompts * kv_dev * pool_count
        n_keys += pool_count * rows_dev
        later += [
            pltpu.VMEM((kv_dev, pool_count, prompts, rows_dev, 2 * HD), jnp.bfloat16),
            pltpu.VMEM((kv_dev, prompts, pool_count * rows_dev, HD), jnp.bfloat16),
            pltpu.VMEM((kv_dev, prompts, pool_count * rows_dev, 2 * HD), jnp.bfloat16),
        ]
    if state is not None:
        operands.append(state)
        copies += kv_dev
        later.append(pltpu.VMEM(state_shape, jnp.float32))
    specs = [SMEM()] * 3 + [ANY()] * (len(operands) - 3)
    if final:
        operands += [which, out_w]
        specs += [SMEM(), ANY()]
        copies += WEIGHT_PARTS
        later.append(pltpu.VMEM((features, width), jnp.bfloat16))
        out_shape = [jax.ShapeDtypeStruct((rows_dev, features), jnp.bfloat16)] * prompts
        out_shape += [jax.ShapeDtypeStruct((rows_dev, width), jnp.bfloat16)] * prompts
    else:
        out_shape = [jax.ShapeDtypeStruct(state_shape, jnp.float32)]
    rows = prompts * rows_dev * kv_dev * group
    return pl.pallas_call(
        functools.partial(
            attend_kernel,
            which_prompts,
            n_chunks,
            pool_count,
            kv_dev,
            [len(chunk) for chunk in chunks],
            span is not None,
            state is not None,
            final,
            block_heads,
        ),
        out_shape=out_shape,
        in_specs=specs,
        out_specs=[VMEM()] * len(out_shape),
        scratch_shapes=scratch + [pltpu.SemaphoreType.DMA((copies,))] + later,
        compiler_params=pltpu.CompilerParams(vmem_limit_bytes=VMEM_LIMIT),
        cost_estimate=pl.CostEstimate(
            flops=rows * n_keys * HD * 6 + 2 * prompts * rows_dev * features * width,
            bytes_accessed=16 << 20,
            transcendentals=rows * n_keys,
        ),
        name="attend",
    )(*operands)


def project_kernel(which, *refs):
    *attended, weight, out = refs
    together = jnp.concatenate([ref[...] for ref in attended], axis=0)
    out[0] = jnp.dot(together, weight[...], preferred_element_type=jnp.float32).astype(out.dtype)


def project(which, skipped, attended, out_w, width):
    rows_dev, depth = attended[0].shape
    rows = rows_dev * len(attended)
    tile = min(1024, width)
    steps = width // tile
    count = which.shape[0] - skipped
    return pl.pallas_call(
        project_kernel,
        grid_spec=pltpu.PrefetchScalarGridSpec(
            num_scalar_prefetch=1,
            grid=(count, steps),
            in_specs=[
                pl.BlockSpec((rows_dev, depth), lambda i, j, which: (0, 0)) for _ in attended
            ]
            + [
                pl.BlockSpec((depth, tile), lambda i, j, which: (0, which[i + skipped] * steps + j)),
            ],
            out_specs=pl.BlockSpec((1, rows, tile), lambda i, j, which: (i, 0, j)),
        ),
        out_shape=jax.ShapeDtypeStruct((count, rows, width), jnp.bfloat16),
        compiler_params=pltpu.CompilerParams(vmem_limit_bytes=VMEM_LIMIT),
        cost_estimate=pl.CostEstimate(
            flops=2 * rows * depth * width * count,
            bytes_accessed=(2 * depth + 4 * rows) * width * count,
            transcendentals=0,
        ),
        name="project",
    )(which, *attended, out_w)


def add_kernel(with_begun, which, partial, *refs):
    total = partial[0].astype(jnp.float32)
    if with_begun:
        total = jnp.where(which[0] < 0, refs[0][...].astype(jnp.float32), total)
    for ref in refs[with_begun:-1]:
        total += ref[...].astype(jnp.float32)
    refs[-1][...] = total.astype(refs[-1].dtype)


def add(which, partials, prompt, came, begun=None):
    rows, width = came[0].shape
    spec = pl.BlockSpec((rows, width), lambda i, which: (0, 0))
    others = ([] if begun is None else [begun]) + came
    return pl.pallas_call(
        functools.partial(add_kernel, int(begun is not None)),
        grid_spec=pltpu.PrefetchScalarGridSpec(
            num_scalar_prefetch=1,
            grid=(1,),
            in_specs=[
                pl.BlockSpec(
                    (1, rows, width), lambda i, which: (jnp.maximum(which[0], 0), prompt, 0)
                )
            ]
            + [spec] * len(others),
            out_specs=spec,
        ),
        out_shape=jax.ShapeDtypeStruct((rows, width), jnp.bfloat16),
        compiler_params=pltpu.CompilerParams(vmem_limit_bytes=VMEM_LIMIT),
        cost_estimate=pl.CostEstimate(
            flops=rows * width, bytes_accessed=8 * rows * width, transcendentals=0
        ),
        name="add",
    )(which.reshape(1), partials, *others)


def over_pool(array, pool_count, after=None):
    gathered = []
    swap = [(i, i ^ 1) for i in range(pool_count)]
    for chips in range(pool_count // 2):
        pairs = [(i, (i + 2 * chips) % pool_count) for i in range(pool_count)]
        arrived = array if chips == 0 else lax.ppermute(array, "pool", pairs)
        passed = arrived
        if after is not None and chips > 0:
            passed, _ = lax.optimization_barrier((arrived, after))
        gathered += [arrived, lax.ppermute(passed, "pool", swap)]
    return gathered


def local(
    queries, span_kv, prefix_pool, hit_blocks, prefix_len, dest_blocks, out_w, residual, norm_gain
):
    tp_count = lax.axis_size("tp")
    tp_index = lax.axis_index("tp")
    pool_count = lax.axis_size("pool")
    pool_index = lax.axis_index("pool")
    prompts, rows_dev = queries.shape[:2]
    heads_dev = queries.shape[2] // HD
    kv_dev = max(1, heads_dev // (QH // KVH))
    slots_dev, block_rows = prefix_pool.shape[:2]
    d_dev = residual.shape[2]
    place = jnp.stack([pool_index, tp_index]).astype(jnp.int32)

    counts, needed, sends = prepare(
        tp_count, pool_count, heads_dev, kv_dev, hit_blocks, prefix_len, place, prefix_pool
    )
    span_own, own_rows = span_parts(heads_dev, kv_dev, block_rows, place, span_kv)
    order = sorted(range(1, tp_count), key=lambda s: -min(s, tp_count - s))
    chunks = [[over_pool(sends[0], pool_count)]]
    span = over_pool(span_own, pool_count)
    along, across = None, [chunks[0][0][2]]
    for at, shift in enumerate(order):
        pairs = [(i, (i + shift) % tp_count) for i in range(tp_count)]
        block = sends[shift]
        if at > 0:
            block, _ = lax.optimization_barrier((block, (along, across[at - 1])))
        along = lax.ppermute(block, "tp", pairs)
        passed, _ = lax.optimization_barrier((along, across[at] if at > 0 else span[2]))
        chunks.append([over_pool(passed, pool_count)])
        across.append(chunks[-1][0][2])

    last = tp_count - 1
    down = tp_index < tp_count // 2
    outs = attend(
        tuple(range(prompts)),
        place,
        prefix_len,
        counts,
        queries,
        chunks,
        kv_dev,
        span=span,
        out_w=out_w,
        which=needed,
        width=d_dev,
    )
    attended, came = outs[:prompts], outs[prompts:]

    def right_pairs(step):
        return [(i, i + 1) for i in range(last) if step >= i + 1]

    def left_pairs(step):
        return [(i, i - 1) for i in range(1, tp_count) if step >= tp_count - i]

    def is_single(step):
        return not {i for i, _ in right_pairs(step)} & {i for i, _ in left_pairs(step)}

    def send(to_right, to_left, step):
        right, left = right_pairs(step), left_pairs(step)
        if to_right is to_left and not {t for _, t in right} & {t for _, t in left}:
            return [lax.ppermute(to_right, "tp", right + left)]
        return [lax.ppermute(to_right, "tp", right), lax.ppermute(to_left, "tp", left)]

    written = lax.all_gather(own_rows[:, None], "pool", axis=1, tiled=True)
    written = written.reshape(-1, block_rows, KVH, 2 * HD)
    targets = dest_blocks.reshape(-1)
    slot_ids = pool_index * slots_dev + jnp.arange(slots_dev)
    matching = (targets[None, :] == slot_ids[:, None]).astype(jnp.int32)
    present = jnp.sum(matching, axis=1) > 0
    source = jnp.sum(matching * jnp.arange(targets.shape[0])[None, :], axis=1)
    new_pool = jnp.where(
        present[:, None, None, None], jnp.take(written, source, axis=0), prefix_pool
    )

    partials = project(needed, 1, attended, out_w, d_dev)
    begun, came = came, [send(block, block, 1) for block in came]
    for step in range(2, tp_count):
        main, other = step - 2, tp_count - step - 2
        for prompt in range(prompts):
            if step == tp_count - 1 and prompt == 0:
                came[0], new_pool = lax.optimization_barrier((came[0], new_pool))
            if is_single(step):
                block = add(jnp.int32(main), partials, prompt, came[prompt])
                came[prompt] = send(block, block, step)
                continue
            to_right, to_left = [
                add(
                    jnp.where(ours, main, other).astype(jnp.int32),
                    partials,
                    prompt,
                    [arrived],
                    begun[prompt] if other < 0 else None,
                )
                for ours, arrived in zip((down, ~down), came[prompt])
            ]
            came[prompt] = send(to_right, to_left, step)

    hidden = jnp.stack(
        [
            (
                partials[tp_count - 2, prompt * rows_dev : (prompt + 1) * rows_dev].astype(jnp.float32)
                + came[prompt][0].astype(jnp.float32)
                + came[prompt][1].astype(jnp.float32)
                + residual[prompt].astype(jnp.float32)
            ).astype(jnp.bfloat16)
            for prompt in range(prompts)
        ]
    )
    hidden = lax.optimization_barrier(hidden)
    widened = hidden.astype(jnp.float32)
    squares = jnp.sum(widened * widened, axis=2)
    total = squares
    for shift in range(1, tp_count):
        pairs = [(i, (i + shift) % tp_count) for i in range(tp_count)]
        total = total + lax.ppermute(squares, "tp", pairs)
    mean_square = total / (d_dev * tp_count)
    normed = (
        widened
        * lax.rsqrt(mean_square + epsilon)[..., None]
        * norm_gain.astype(jnp.float32)[None, None, :]
    ).astype(jnp.bfloat16)
    return hidden, normed, new_pool


def solution(mesh):
    placed = (
        P("groups", "pool", "tp"),
        P("groups", "pool", None, None),
        P(("groups", "pool"), "tp", None, None),
        P("groups", None),
        P("groups"),
        P("groups", None),
        P("tp", None),
        P("groups", "pool", "tp"),
        P("tp"),
    )
    return jax.shard_map(
        local,
        mesh=mesh,
        in_specs=placed,
        out_specs=(
            P("groups", "pool", "tp"),
            P("groups", "pool", "tp"),
            P(("groups", "pool"), "tp", None, None),
        ),
        check_vma=False,
    )
```

time: 240 us -> 194 us (0.81)
  waiting for transfers between devices: 87 us -> 58.7 us
  Pallas kernels: 72.5 us -> 62.8 us
  local copies, waits for them, and re-layouts: 8.15 us -> 4.39 us
  other arithmetic: 11.6 us -> 8.3 us
    ppermute x25 -> x23, waiting for transfers between devices: 69.4 us -> 20.7 us  [the longest x4 6.78 us: send(): lax.ppermute(to_left, 'tp', left)]
    pallas_call x5 -> x1, Pallas kernels: 34.1 us -> 14.4 us  [project(): pl.pallas_call(project_kernel, grid_spec=pltpu.PrefetchScalarGridSpec(num...]
    ppermute x5, waiting for transfers between devices: 17.6 us -> 34.4 us  [over_pool(): arrived = array if chips == 0 else lax.ppermute(array, 'pool', pairs)]
    pallas_call x2 -> x8, Pallas kernels: 33.1 us -> 43.4 us  [the longest x1 27.5 us: attend(): pl.pallas_call(functools.partial(attend_kernel, which_prompts, n_chunks,...]
    convert_element_type x3 -> x0, other arithmetic: 4.67 us -> none  [local(): (mine + came[prompt].astype(jnp.float32)).astype(jnp.bfloat16)]
    ppermute x3, waiting for transfers between devices: 0.01 us -> 3.62 us  [local(): total = total + lax.ppermute(squares, 'tp', pairs)]
    ppermute x25 -> x23, starting transfers between devices: 36 us -> 33.1 us  [the longest x4 16.4 us: send(): lax.ppermute(to_right, 'tp', right)]
  transfers between devices with their start and end apart: 34 -> 32, of which waited for: 10 -> 15; matrix products, arithmetic and copies ran while one was open for 6% -> 3% of each run, Pallas kernels for 28% -> 30%
where the time goes in v2:
time: 194 us; the launch traced here: 193 us
  Pallas kernels  62.8 us (32%)
  waiting for transfers between devices  58.7 us (30%)
  starting transfers between devices  44.2 us (23%)
  between operations  14.4 us (7%)
  other arithmetic  8.3 us (4%)
  local copies, waits for them, and re-layouts  4.39 us (2%)
    ppermute x5, waiting for transfers between devices, over_pool(): arrived = array if chips == 0 else lax.ppermute(array, 'pool', pairs)  34.4 us
    pallas_call x1, Pallas kernels, attend(): pl.pallas_call(functools.partial(attend_kernel, which_prompts, n_chunks,...  27.5 us
    ppermute x4, starting transfers between devices, send(): lax.ppermute(to_right, 'tp', right)  16.4 us
    pallas_call x1, Pallas kernels, project(): pl.pallas_call(project_kernel, grid_spec=pltpu.PrefetchScalarGridSpec(num...  14.4 us
    pallas_call x6, Pallas kernels, add(): pl.pallas_call(functools.partial(add_kernel, int(begun is not None)), gri...  13.6 us
    ppermute x4, waiting for transfers between devices, send(): lax.ppermute(to_left, 'tp', left)  6.78 us
    ppermute x3, starting transfers between devices, local(): along = lax.ppermute(block, 'tp', pairs)  6.62 us
    ppermute x3, waiting for transfers between devices, local(): along = lax.ppermute(block, 'tp', pairs)  5.71 us
  transfers between devices with their start and end apart: 32, of which 15 were waited for; matrix products, arithmetic and copies ran while one was open for 3% of the time, Pallas kernels for 30%

profile of v2, /device:TPU:0, one launch (start us, length us, event | category | flops | bytes accessed | tf_op | source)
XLA Modules:
  0.0 192.9 jit_solution(12822194615712018167)
XLA Ops:
  7.9 5.1 %prepare.1 = (s32[2,4]{1,0:T(2,128)}, s32[4]{0:T(128)}, bf16[12,2,32,256]{3,2,1,0:T(8,128)(2,1)}, bf16[12,2,32,256]{3,2,1,0:T(8,128)(2,1)}, bf16[12,2,32,256]{3,...) custom-call(s32[2,24]{1,0:T(2,128)} %hit.1, s32[2]{0:T(128)} %refs_1_.1, s32[2]{0:T(128)} %pad_add_fusion.place.refs_0_, ...), custom_call_target="tpu_custom_call" | custom-call | bytes 8388608 | tf_op jit(solution)/shard_map/prepare/pallas_call | solution.py:107
  13.0 4.1 %collective-permute-start.3 = (bf16[12,2,32,256]{3,2,1,0:T(8,128)(2,1)}, bf16[12,2,32,256]{3,2,1,0:T(8,128)(2,1)S(1)}, u32[]{:S(2)}, u32[]{:S(2)}) collective-permute-start(bf16[12,2,32,256]{3,2,1,0:T(8,128)(2,1)} %get-tuple-element.26), channel_id=1, source_target_pairs={{0,2},{1,3},{2,0},{3,1},{4,6},{5,7},{6,4},{7,5},{8,10},{9,11},{10,... | collective-permute-start | bytes 1179656 | tf_op jit(solution)/shard_map/ppermute | solution.py:550
  18.6 2.2 %span_parts.1 = (bf16[2,2,128,256]{3,2,1,0:T(8,128)(2,1)}, bf16[2,32,8,256]{3,2,1,0:T(8,128)(2,1)}) custom-call(s32[2]{0:T(128)} %pad_add_fusion.place.refs_0_, bf16[2,128,8,256]{3,2,1,0:T(8,128)(2,1)} %span.1), custom_call_target="tpu_custom_call" | custom-call | bytes 2097152 | tf_op jit(solution)/shard_map/span_parts/pallas_call | solution.py:143
  21.4 12.2 %collective-permute-done.4.refs_22_ = bf16[2,2,128,256]{3,2,1,0:T(8,128)(2,1)} collective-permute-done((bf16[2,2,128,256]{3,2,1,0:T(8,128)(2,1)}, bf16[2,2,128,256]{3,2,1,0:T(8,128)(2,1)}, u32[]{:S(2)}, u32[]{:S(2)}) %collective-permute-start.4) | collective-permute-done | bytes 262176 | tf_op jit(solution)/shard_map/ppermute | solution.py:515
  34.8 1.5 collective-permute-start.6
  37.2 8.0 %collective-permute-done.6.refs_10_ = bf16[12,2,32,256]{3,2,1,0:T(8,128)(2,1)S(1)} collective-permute-done((bf16[12,2,32,256]{3,2,1,0:T(8,128)(2,1)S(1)}, bf16[12,2,32,256]{3,2,1,0:T(8,128)(2,1)S(1)}, u32[]{:S(2)}, u32[]{:S(2)}) %collective-permute-start.6) | collective-permute-done | bytes 393248 | tf_op jit(solution)/shard_map/ppermute | solution.py:515
  45.1 4.0 %collective-permute-done.8.refs_12_ = bf16[12,2,32,256]{3,2,1,0:T(8,128)(2,1)S(1)} collective-permute-done((bf16[12,2,32,256]{3,2,1,0:T(8,128)(2,1)}, bf16[12,2,32,256]{3,2,1,0:T(8,128)(2,1)S(1)}, u32[]{:S(2)}, u32[]{:S(2)}) %collective-permute-start.8) | collective-permute-done | bytes 393248 | tf_op jit(solution)/shard_map/ppermute | solution.py:550
  49.6 1.7 collective-permute-start.12
  51.9 7.0 %collective-permute-done.10.refs_14_ = bf16[12,2,32,256]{3,2,1,0:T(8,128)(2,1)S(1)} collective-permute-done((bf16[12,2,32,256]{3,2,1,0:T(8,128)(2,1)S(1)}, bf16[12,2,32,256]{3,2,1,0:T(8,128)(2,1)S(1)}, u32[]{:S(2)}, u32[]{:S(2)}) %collective-permute-start.10) | collective-permute-done | bytes 393248 | tf_op jit(solution)/shard_map/ppermute | solution.py:515
  63.4 7.1 %collective-permute-done.14.refs_18_ = bf16[12,2,32,256]{3,2,1,0:T(8,128)(2,1)} collective-permute-done((bf16[12,2,32,256]{3,2,1,0:T(8,128)(2,1)S(1)}, bf16[12,2,32,256]{3,2,1,0:T(8,128)(2,1)}, u32[]{:S(2)}, u32[]{:S(2)}) %collective-permute-start.14) | collective-permute-done | bytes 393248 | tf_op jit(solution)/shard_map/ppermute | solution.py:515
  70.6 1.8 collective-permute-done.15.refs_19_
  73.3 27.5 %attend.1 = (bf16[128,2048]{1,0:T(8,128)(2,1)}, bf16[128,2048]{1,0:T(8,128)(2,1)}, bf16[128,2048]{1,0:T(8,128)(2,1)}, bf16[128,2048]{1,0:T(8,128)(2,1)}) custom-call(s32[2]{0:T(128)} %pad_add_fusion.place.refs_0_, s32[2]{0:T(128)} %refs_1_.1, s32[2,4]{1,0:T(2,128)} %get-tuple-element.24.refs_2_, bf16[2,128,2048]{2,1,0:T(8,128)(2,1)} %refs_3_.1, ...), custom_call_target="tpu_custom_call" | custom-call | flops 13421772800 | bytes 16777216 | tf_op jit(solution)/shard_map/attend/pallas_call | solution.py:412
  103.4 14.4 %project.1.partial = bf16[3,256,2048]{2,1,0:T(8,128)(2,1)} custom-call(s32[4]{0:T(128)} %get-tuple-element.23.refs_24_.which, bf16[128,2048]{1,0:T(8,128)(2,1)} %get-tuple-element.35.refs_0_, bf16[128,2048]{1,0:T(8,128)(2,1)} %get-tuple-element.36.refs_1_, bf16[2048,8192]{1,0:T(8,128)(2,1)} %refs_2_.1), custom_call_target="tpu_custom_call" | custom-call | flops 6442450944 | bytes 31457280 | tf_op jit(solution)/shard_map/project/pallas_call | solution.py:451
  118.6 2.1 %add.128 = bf16[128,2048]{1,0:T(8,128)(2,1)} custom-call(s32[1]{0:T(128)} %constant.12.clone.1.which, bf16[3,256,2048]{2,1,0:T(8,128)(2,1)} %project.1.partial, bf16[128,2048]{1,0:T(8,128)(2,1)} %copy-done.3), custom_call_target="tpu_custom_call" | custom-call | flops 262144 | bytes 2097152 | tf_op jit(solution)/shard_map/add/pallas_call | solution.py:488
  120.7 2.1 %collective-permute-start.19 = (bf16[128,2048]{1,0:T(8,128)(2,1)}, bf16[128,2048]{1,0:T(8,128)(2,1)}, u32[]{:S(2)}, u32[]{:S(2)}) collective-permute-start(bf16[128,2048]{1,0:T(8,128)(2,1)} %add.128), channel_id=1, source_target_pairs={{0,1},{1,2},{4,5},{5,6},{8,9},{9,10},{12,13},{13,14},{16,17},{17,1... | collective-permute-start | bytes 1572872 | tf_op jit(solution)/shard_map/ppermute | solution.py:585
  124.3 1.5 collective-permute-done.23.refs_0_
  126.6 2.1 %add.131 = bf16[128,2048]{1,0:T(8,128)(2,1)} custom-call(s32[1]{0:T(128)} %constant.12.clone.1.which, bf16[3,256,2048]{2,1,0:T(8,128)(2,1)} %project.1.partial, bf16[128,2048]{1,0:T(8,128)(2,1)} %copy-done.2), custom_call_target="tpu_custom_call" | custom-call | flops 262144 | bytes 2097152 | tf_op jit(solution)/shard_map/add/pallas_call | solution.py:488
  130.2 4.9 %collective-permute-start.24 = (bf16[128,2048]{1,0:T(8,128)(2,1)}, bf16[128,2048]{1,0:T(8,128)(2,1)}, u32[]{:S(2)}, u32[]{:S(2)}) collective-permute-start(bf16[128,2048]{1,0:T(8,128)(2,1)} %add.131), channel_id=1, source_target_pairs={{0,1},{1,2},{4,5},{5,6},{8,9},{9,10},{12,13},{13,14},{16,17},{17,1... | collective-permute-start | bytes 1572872 | tf_op jit(solution)/shard_map/ppermute | solution.py:585
  135.1 2.0 %gather_fusion = bf16[24,32,8,256]{3,2,1,0:T(8,128)(2,1)S(1)} fusion(bf16[8,32,8,256]{3,2,1,0:T(8,128)(2,1)} %bitcast.29, s32[1024]{0:T(1024)S(1)} %pad_clamp_fusion), kind=kCustom, calls=%fused_computation | custom fusion | bytes 6291552 | tf_op jit(solution)/shard_map/jit(_take)/gather | solution.py:595
  137.1 4.0 %select_select_fusion = bf16[24,32,8,256]{3,2,1,0:T(8,128)(2,1)} fusion(bf16[24,32,8,256]{3,2,1,0:T(8,128)(2,1)} %pool.1, bf16[24,32,8,256]{3,2,1,0:T(8,128)(2,1)S(1)} %gather_fusion, pred[24]{0:T(512)(128)(4,1)S(1)} %get-tuple-element.47, pred[24]{0:T(512)(128)(4,1)S(1)} %get-tuple-element.48), kind=kLoop, calls=%fused_computation.1 | loop fusion | flops 3145728 | bytes 9437232 | tf_op jit(solution)/shard_map/jit(_where)/select_n | solution.py:594
  141.1 2.3 %add.130 = bf16[128,2048]{1,0:T(8,128)(2,1)} custom-call(s32[1]{0:T(128)} %bitcast.7.which, bf16[3,256,2048]{2,1,0:T(8,128)(2,1)} %project.1.partial, bf16[128,2048]{1,0:T(8,128)(2,1)} %get-tuple-element.37.refs_0_, bf16[128,2048]{1,0:T(8,128)(2,1)} %collective-permute-done.20.refs_1_), custom_call_target="tpu_custom_call" | custom-call | flops 262144 | bytes 2097152 | tf_op jit(solution)/shard_map/add/pallas_call | solution.py:488
  144.7 2.3 %add.129 = bf16[128,2048]{1,0:T(8,128)(2,1)} custom-call(s32[1]{0:T(128)} %bitcast.3.which, bf16[3,256,2048]{2,1,0:T(8,128)(2,1)} %project.1.partial, bf16[128,2048]{1,0:T(8,128)(2,1)} %get-tuple-element.37.refs_0_, bf16[128,2048]{1,0:T(8,128)(2,1)} %collective-permute-done.19.refs_1_), custom_call_target="tpu_custom_call" | custom-call | flops 262144 | bytes 2097152 | tf_op jit(solution)/shard_map/add/pallas_call | solution.py:488
  147.1 4.7 %collective-permute-start.21 = (bf16[128,2048]{1,0:T(8,128)(2,1)}, bf16[128,2048]{1,0:T(8,128)(2,1)S(1)}, u32[]{:S(2)}, u32[]{:S(2)}) collective-permute-start(bf16[128,2048]{1,0:T(8,128)(2,1)} %add.129), channel_id=1, source_target_pairs={{0,1},{1,2},{2,3},{4,5},{5,6},{6,7},{8,9},{9,10},{10,11},{12,13},{... | collective-permute-start | bytes 1572872 | tf_op jit(solution)/shard_map/ppermute | solution.py:585
  151.8 2.4 %add.133 = bf16[128,2048]{1,0:T(8,128)(2,1)} custom-call(s32[1]{0:T(128)} %bitcast.7.which, bf16[3,256,2048]{2,1,0:T(8,128)(2,1)} %project.1.partial, bf16[128,2048]{1,0:T(8,128)(2,1)} %get-tuple-element.41.refs_0_, bf16[128,2048]{1,0:T(8,128)(2,1)} %collective-permute-done.26.refs_1_), custom_call_target="tpu_custom_call" | custom-call | flops 262144 | bytes 2097152 | tf_op jit(solution)/shard_map/add/pallas_call | solution.py:488
  155.6 2.3 %add.132 = bf16[128,2048]{1,0:T(8,128)(2,1)} custom-call(s32[1]{0:T(128)} %bitcast.3.which, bf16[3,256,2048]{2,1,0:T(8,128)(2,1)} %project.1.partial, bf16[128,2048]{1,0:T(8,128)(2,1)} %get-tuple-element.41.refs_0_, bf16[128,2048]{1,0:T(8,128)(2,1)} %collective-permute-done.24.refs_1_), custom_call_target="tpu_custom_call" | custom-call | flops 262144 | bytes 2097152 | tf_op jit(solution)/shard_map/add/pallas_call | solution.py:488
  157.9 4.7 %collective-permute-start.25 = (bf16[128,2048]{1,0:T(8,128)(2,1)}, bf16[128,2048]{1,0:T(8,128)(2,1)S(1)}, u32[]{:S(2)}, u32[]{:S(2)}) collective-permute-start(bf16[128,2048]{1,0:T(8,128)(2,1)} %add.132), channel_id=1, source_target_pairs={{0,1},{1,2},{2,3},{4,5},{5,6},{6,7},{8,9},{9,10},{10,11},{12,13},{... | collective-permute-start | bytes 1572872 | tf_op jit(solution)/shard_map/ppermute | solution.py:585
  162.8 6.8 %collective-permute-done.27 = bf16[128,2048]{1,0:T(8,128)(2,1)S(1)} collective-permute-done((bf16[128,2048]{1,0:T(8,128)(2,1)}, bf16[128,2048]{1,0:T(8,128)(2,1)S(1)}, u32[]{:S(2)}, u32[]{:S(2)}) %collective-permute-start.27) | collective-permute-done | bytes 524320 | tf_op jit(solution)/shard_map/ppermute | solution.py:585
  169.6 3.6 %collective-permute-done.25 = bf16[128,2048]{1,0:T(8,128)(2,1)S(1)} collective-permute-done((bf16[128,2048]{1,0:T(8,128)(2,1)}, bf16[128,2048]{1,0:T(8,128)(2,1)S(1)}, u32[]{:S(2)}, u32[]{:S(2)}) %collective-permute-start.25) | collective-permute-done | bytes 524320 | tf_op jit(solution)/shard_map/ppermute | solution.py:585
  173.2 1.9 fusion.7
  175.5 3.3 %collective-permute-start.30 = (f32[2,128]{1,0:T(2,128)S(1)}, f32[2,128]{1,0:T(2,128)S(1)}, u32[]{:S(2)}, u32[]{:S(2)}) collective-permute-start(f32[2,128]{1,0:T(2,128)S(1)} %fusion), channel_id=1, source_target_pairs={{0,3},{1,0},{2,1},{3,2},{4,7},{5,4},{6,5},{7,6},{8,11},{9,8},{10,9... | collective-permute-start | bytes 3080 | tf_op jit(solution)/shard_map/ppermute | solution.py:638
  179.3 1.7 collective-permute-start.28
  181.1 2.2 %collective-permute-done.29 = f32[2,128]{1,0:T(2,128)S(1)} collective-permute-done((f32[2,128]{1,0:T(2,128)S(1)}, f32[2,128]{1,0:T(2,128)S(1)}, u32[]{:S(2)}, u32[]{:S(2)}) %collective-permute-start.29) | collective-permute-done | bytes 1056 | tf_op jit(solution)/shard_map/ppermute | solution.py:638
  (98 shorter events, 24.8 us)
Async XLA Ops:
  7.2 127.9 %all-gather.3.cloned.1.call-start = ((), (), s32[]{:S(2)}) async-start(), calls=%async_computation | async-start | bytes 1310720 | tf_op jit(solution)/shard_map/all_gather | solution.py:587
  13.0 21.9 %collective-permute-start.3 = (bf16[12,2,32,256]{3,2,1,0:T(8,128)(2,1)}, bf16[12,2,32,256]{3,2,1,0:T(8,128)(2,1)S(1)}, u32[]{:S(2)}, u32[]{:S(2)}) collective-permute-start(bf16[12,2,32,256]{3,2,1,0:T(8,128)(2,1)} %get-tuple-element.26), channel_id=1, source_target_pairs={{0,2},{1,3},{2,0},{3,1},{4,6},{5,7},{6,4},{7,5},{8,10},{9,11},{10,... | collective-permute-start | bytes 1179656 | tf_op jit(solution)/shard_map/ppermute | solution.py:550
  17.1 19.3 %collective-permute-start.1 = (bf16[12,2,32,256]{3,2,1,0:T(8,128)(2,1)}, bf16[12,2,32,256]{3,2,1,0:T(8,128)(2,1)S(1)}, u32[]{:S(2)}, u32[]{:S(2)}) collective-permute-start(bf16[12,2,32,256]{3,2,1,0:T(8,128)(2,1)} %get-tuple-element.25.refs_4_), channel_id=1, source_target_pairs={{0,8},{4,12},{8,0},{12,4},{1,9},{5,13},{9,1},{13,5},{2,10},{6,14},... | collective-permute-start | bytes 1179656 | tf_op jit(solution)/shard_map/ppermute | solution.py:515
  20.8 12.8 %collective-permute-start.4 = (bf16[2,2,128,256]{3,2,1,0:T(8,128)(2,1)}, bf16[2,2,128,256]{3,2,1,0:T(8,128)(2,1)}, u32[]{:S(2)}, u32[]{:S(2)}) collective-permute-start(bf16[2,2,128,256]{3,2,1,0:T(8,128)(2,1)} %get-tuple-element.27.refs_20_), channel_id=1, source_target_pairs={{0,8},{4,12},{8,0},{12,4},{1,9},{5,13},{9,1},{13,5},{2,10},{6,14},... | collective-permute-start | bytes 786440 | tf_op jit(solution)/shard_map/ppermute | solution.py:515
  34.8 10.3 %collective-permute-start.6 = (bf16[12,2,32,256]{3,2,1,0:T(8,128)(2,1)S(1)}, bf16[12,2,32,256]{3,2,1,0:T(8,128)(2,1)S(1)}, u32[]{:S(2)}, u32[]{:S(2)}) collective-permute-start(bf16[12,2,32,256]{3,2,1,0:T(8,128)(2,1)S(1)} %collective-permute-done.3.refs_8_), channel_id=1, source_target_pairs={{0,8},{4,12},{8,0},{12,4},{1,9},{5,13},{9,1},{13,5},{2,10},{6,14},... | collective-permute-start | bytes 1179656 | tf_op jit(solution)/shard_map/ppermute | solution.py:515
  36.4 12.7 %collective-permute-start.8 = (bf16[12,2,32,256]{3,2,1,0:T(8,128)(2,1)}, bf16[12,2,32,256]{3,2,1,0:T(8,128)(2,1)S(1)}, u32[]{:S(2)}, u32[]{:S(2)}) collective-permute-start(bf16[12,2,32,256]{3,2,1,0:T(8,128)(2,1)} %get-tuple-element.30), channel_id=1, source_target_pairs={{0,1},{1,2},{2,3},{3,0},{4,5},{5,6},{6,7},{7,4},{8,9},{9,10},{10,1... | collective-permute-start | bytes 1179656 | tf_op jit(solution)/shard_map/ppermute | solution.py:550
  49.1 9.8 %collective-permute-start.10 = (bf16[12,2,32,256]{3,2,1,0:T(8,128)(2,1)S(1)}, bf16[12,2,32,256]{3,2,1,0:T(8,128)(2,1)S(1)}, u32[]{:S(2)}, u32[]{:S(2)}) collective-permute-start(bf16[12,2,32,256]{3,2,1,0:T(8,128)(2,1)S(1)} %collective-permute-done.8.refs_12_), channel_id=1, source_target_pairs={{0,8},{4,12},{8,0},{12,4},{1,9},{5,13},{9,1},{13,5},{2,10},{6,14},... | collective-permute-start | bytes 1179656 | tf_op jit(solution)/shard_map/ppermute | solution.py:515
  49.6 9.8 %collective-permute-start.12 = (bf16[12,2,32,256]{3,2,1,0:T(8,128)(2,1)}, bf16[12,2,32,256]{3,2,1,0:T(8,128)(2,1)S(1)}, u32[]{:S(2)}, u32[]{:S(2)}) collective-permute-start(bf16[12,2,32,256]{3,2,1,0:T(8,128)(2,1)} %get-tuple-element.33), channel_id=1, source_target_pairs={{0,3},{1,0},{2,1},{3,2},{4,7},{5,4},{6,5},{7,6},{8,11},{9,8},{10,9... | collective-permute-start | bytes 1179656 | tf_op jit(solution)/shard_map/ppermute | solution.py:550
  51.4 9.5 %collective-permute-start.16 = (bf16[2,2,128,256]{3,2,1,0:T(8,128)(2,1)}, bf16[2,2,128,256]{3,2,1,0:T(8,128)(2,1)}, u32[]{:S(2)}, u32[]{:S(2)}) collective-permute-start(bf16[2,2,128,256]{3,2,1,0:T(8,128)(2,1)} %get-tuple-element.27.refs_20_), channel_id=1, source_target_pairs={{0,4},{4,0},{8,12},{12,8},{1,5},{5,1},{9,13},{13,9},{2,6},{6,2},{1... | collective-permute-start | bytes 786440 | tf_op jit(solution)/shard_map/ppermute | solution.py:519
  51.4 9.7 %collective-permute-start = (bf16[12,2,32,256]{3,2,1,0:T(8,128)(2,1)}, bf16[12,2,32,256]{3,2,1,0:T(8,128)(2,1)S(1)}, u32[]{:S(2)}, u32[]{:S(2)}) collective-permute-start(bf16[12,2,32,256]{3,2,1,0:T(8,128)(2,1)} %get-tuple-element.25.refs_4_), channel_id=1, source_target_pairs={{0,4},{4,0},{8,12},{12,8},{1,5},{5,1},{9,13},{13,9},{2,6},{6,2},{1... | collective-permute-start | bytes 1179656 | tf_op jit(solution)/shard_map/ppermute | solution.py:519
  51.9 11.4 %collective-permute-start.5 = (bf16[12,2,32,256]{3,2,1,0:T(8,128)(2,1)S(1)}, bf16[12,2,32,256]{3,2,1,0:T(8,128)(2,1)S(1)}, u32[]{:S(2)}, u32[]{:S(2)}) collective-permute-start(bf16[12,2,32,256]{3,2,1,0:T(8,128)(2,1)S(1)} %collective-permute-done.3.refs_8_), channel_id=1, source_target_pairs={{0,4},{4,0},{8,12},{12,8},{1,5},{5,1},{9,13},{13,9},{2,6},{6,2},{1... | collective-permute-start | bytes 1179656 | tf_op jit(solution)/shard_map/ppermute | solution.py:519
  58.9 4.0 %collective-permute-start.2 = (bf16[12,2,32,256]{3,2,1,0:T(8,128)(2,1)S(1)}, bf16[12,2,32,256]{3,2,1,0:T(8,128)(2,1)S(1)}, u32[]{:S(2)}, u32[]{:S(2)}) collective-permute-start(bf16[12,2,32,256]{3,2,1,0:T(8,128)(2,1)S(1)} %collective-permute-done.1.refs_6_), channel_id=1, source_target_pairs={{0,4},{4,0},{8,12},{12,8},{1,5},{5,1},{9,13},{13,9},{2,6},{6,2},{1... | collective-permute-start | bytes 1179656 | tf_op jit(solution)/shard_map/ppermute | solution.py:519
  59.4 11.1 %collective-permute-start.14 = (bf16[12,2,32,256]{3,2,1,0:T(8,128)(2,1)S(1)}, bf16[12,2,32,256]{3,2,1,0:T(8,128)(2,1)}, u32[]{:S(2)}, u32[]{:S(2)}) collective-permute-start(bf16[12,2,32,256]{3,2,1,0:T(8,128)(2,1)S(1)} %collective-permute-done.12.refs_16_), channel_id=1, source_target_pairs={{0,8},{4,12},{8,0},{12,4},{1,9},{5,13},{9,1},{13,5},{2,10},{6,14},... | collective-permute-start | bytes 1179656 | tf_op jit(solution)/shard_map/ppermute | solution.py:515
  60.9 1.9 collective-permute-start.17
  61.1 9.5 %collective-permute-start.9 = (bf16[12,2,32,256]{3,2,1,0:T(8,128)(2,1)S(1)}, bf16[12,2,32,256]{3,2,1,0:T(8,128)(2,1)S(1)}, u32[]{:S(2)}, u32[]{:S(2)}) collective-permute-start(bf16[12,2,32,256]{3,2,1,0:T(8,128)(2,1)S(1)} %collective-permute-done.8.refs_12_), channel_id=1, source_target_pairs={{0,4},{4,0},{8,12},{12,8},{1,5},{5,1},{9,13},{13,9},{2,6},{6,2},{1... | collective-permute-start | bytes 1179656 | tf_op jit(solution)/shard_map/ppermute | solution.py:519
  62.7 7.8 %collective-permute-start.7 = (bf16[12,2,32,256]{3,2,1,0:T(8,128)(2,1)S(1)}, bf16[12,2,32,256]{3,2,1,0:T(8,128)(2,1)S(1)}, u32[]{:S(2)}, u32[]{:S(2)}) collective-permute-start(bf16[12,2,32,256]{3,2,1,0:T(8,128)(2,1)S(1)} %collective-permute-done.6.refs_10_), channel_id=1, source_target_pairs={{0,4},{4,0},{8,12},{12,8},{1,5},{5,1},{9,13},{13,9},{2,6},{6,2},{1... | collective-permute-start | bytes 1179656 | tf_op jit(solution)/shard_map/ppermute | solution.py:519
  62.9 7.7 %collective-permute-start.13 = (bf16[12,2,32,256]{3,2,1,0:T(8,128)(2,1)S(1)}, bf16[12,2,32,256]{3,2,1,0:T(8,128)(2,1)S(1)}, u32[]{:S(2)}, u32[]{:S(2)}) collective-permute-start(bf16[12,2,32,256]{3,2,1,0:T(8,128)(2,1)S(1)} %collective-permute-done.12.refs_16_), channel_id=1, source_target_pairs={{0,4},{4,0},{8,12},{12,8},{1,5},{5,1},{9,13},{13,9},{2,6},{6,2},{1... | collective-permute-start | bytes 1179656 | tf_op jit(solution)/shard_map/ppermute | solution.py:519
  63.3 7.3 %collective-permute-start.11 = (bf16[12,2,32,256]{3,2,1,0:T(8,128)(2,1)S(1)}, bf16[12,2,32,256]{3,2,1,0:T(8,128)(2,1)S(1)}, u32[]{:S(2)}, u32[]{:S(2)}) collective-permute-start(bf16[12,2,32,256]{3,2,1,0:T(8,128)(2,1)S(1)} %collective-permute-done.10.refs_14_), channel_id=1, source_target_pairs={{0,4},{4,0},{8,12},{12,8},{1,5},{5,1},{9,13},{13,9},{2,6},{6,2},{1... | collective-permute-start | bytes 1179656 | tf_op jit(solution)/shard_map/ppermute | solution.py:519
  70.5 1.9 %collective-permute-start.15 = (bf16[12,2,32,256]{3,2,1,0:T(8,128)(2,1)}, bf16[12,2,32,256]{3,2,1,0:T(8,128)(2,1)S(1)}, u32[]{:S(2)}, u32[]{:S(2)}) collective-permute-start(bf16[12,2,32,256]{3,2,1,0:T(8,128)(2,1)} %collective-permute-done.14.refs_18_), channel_id=1, source_target_pairs={{0,4},{4,0},{8,12},{12,8},{1,5},{5,1},{9,13},{13,9},{2,6},{6,2},{1... | collective-permute-start | bytes 1179656 | tf_op jit(solution)/shard_map/ppermute | solution.py:519
  100.7 17.1 %collective-permute-start.18 = (bf16[128,2048]{1,0:T(8,128)(2,1)}, bf16[128,2048]{1,0:T(8,128)(2,1)S(1)}, u32[]{:S(2)}, u32[]{:S(2)}) collective-permute-start(bf16[128,2048]{1,0:T(8,128)(2,1)} %get-tuple-element.37.refs_0_), channel_id=1, source_target_pairs={{0,1},{3,2},{4,5},{7,6},{8,9},{11,10},{12,13},{15,14},{16,17},{19,... | collective-permute-start | bytes 1572872 | tf_op jit(solution)/shard_map/ppermute | solution.py:584
  102.1 23.7 %collective-permute-start.23 = (bf16[128,2048]{1,0:T(8,128)(2,1)}, bf16[128,2048]{1,0:T(8,128)(2,1)S(1)}, u32[]{:S(2)}, u32[]{:S(2)}) collective-permute-start(bf16[128,2048]{1,0:T(8,128)(2,1)} %get-tuple-element.41.refs_0_), channel_id=1, source_target_pairs={{0,1},{3,2},{4,5},{7,6},{8,9},{11,10},{12,13},{15,14},{16,17},{19,... | collective-permute-start | bytes 1572872 | tf_op jit(solution)/shard_map/ppermute | solution.py:584
  120.7 20.4 %collective-permute-start.19 = (bf16[128,2048]{1,0:T(8,128)(2,1)}, bf16[128,2048]{1,0:T(8,128)(2,1)}, u32[]{:S(2)}, u32[]{:S(2)}) collective-permute-start(bf16[128,2048]{1,0:T(8,128)(2,1)} %add.128), channel_id=1, source_target_pairs={{0,1},{1,2},{4,5},{5,6},{8,9},{9,10},{12,13},{13,14},{16,17},{17,1... | collective-permute-start | bytes 1572872 | tf_op jit(solution)/shard_map/ppermute | solution.py:585
  122.8 18.3 %collective-permute-start.20 = (bf16[128,2048]{1,0:T(8,128)(2,1)}, bf16[128,2048]{1,0:T(8,128)(2,1)}, u32[]{:S(2)}, u32[]{:S(2)}) collective-permute-start(bf16[128,2048]{1,0:T(8,128)(2,1)} %add.128), channel_id=1, source_target_pairs={{2,1},{3,2},{6,5},{7,6},{10,9},{11,10},{14,13},{15,14},{18,17},{19... | collective-permute-start | bytes 1572872 | tf_op jit(solution)/shard_map/ppermute | solution.py:585
  128.7 23.0 %collective-permute-start.26 = (bf16[128,2048]{1,0:T(8,128)(2,1)}, bf16[128,2048]{1,0:T(8,128)(2,1)}, u32[]{:S(2)}, u32[]{:S(2)}) collective-permute-start(bf16[128,2048]{1,0:T(8,128)(2,1)} %add.131), channel_id=1, source_target_pairs={{2,1},{3,2},{6,5},{7,6},{10,9},{11,10},{14,13},{15,14},{18,17},{19... | collective-permute-start | bytes 1572872 | tf_op jit(solution)/shard_map/ppermute | solution.py:585
  130.2 25.4 %collective-permute-start.24 = (bf16[128,2048]{1,0:T(8,128)(2,1)}, bf16[128,2048]{1,0:T(8,128)(2,1)}, u32[]{:S(2)}, u32[]{:S(2)}) collective-permute-start(bf16[128,2048]{1,0:T(8,128)(2,1)} %add.131), channel_id=1, source_target_pairs={{0,1},{1,2},{4,5},{5,6},{8,9},{9,10},{12,13},{13,14},{16,17},{17,1... | collective-permute-start | bytes 1572872 | tf_op jit(solution)/shard_map/ppermute | solution.py:585
  143.4 19.2 %collective-permute-start.22 = (bf16[128,2048]{1,0:T(8,128)(2,1)}, bf16[128,2048]{1,0:T(8,128)(2,1)S(1)}, u32[]{:S(2)}, u32[]{:S(2)}) collective-permute-start(bf16[128,2048]{1,0:T(8,128)(2,1)} %add.130), channel_id=1, source_target_pairs={{1,0},{2,1},{3,2},{5,4},{6,5},{7,6},{9,8},{10,9},{11,10},{13,12},{... | collective-permute-start | bytes 1572872 | tf_op jit(solution)/shard_map/ppermute | solution.py:585
  147.1 15.7 %collective-permute-start.21 = (bf16[128,2048]{1,0:T(8,128)(2,1)}, bf16[128,2048]{1,0:T(8,128)(2,1)S(1)}, u32[]{:S(2)}, u32[]{:S(2)}) collective-permute-start(bf16[128,2048]{1,0:T(8,128)(2,1)} %add.129), channel_id=1, source_target_pairs={{0,1},{1,2},{2,3},{4,5},{5,6},{6,7},{8,9},{9,10},{10,11},{12,13},{... | collective-permute-start | bytes 1572872 | tf_op jit(solution)/shard_map/ppermute | solution.py:585
  154.2 15.4 %collective-permute-start.27 = (bf16[128,2048]{1,0:T(8,128)(2,1)}, bf16[128,2048]{1,0:T(8,128)(2,1)S(1)}, u32[]{:S(2)}, u32[]{:S(2)}) collective-permute-start(bf16[128,2048]{1,0:T(8,128)(2,1)} %add.133), channel_id=1, source_target_pairs={{1,0},{2,1},{3,2},{5,4},{6,5},{7,6},{9,8},{10,9},{11,10},{13,12},{... | collective-permute-start | bytes 1572872 | tf_op jit(solution)/shard_map/ppermute | solution.py:585
  157.9 15.2 %collective-permute-start.25 = (bf16[128,2048]{1,0:T(8,128)(2,1)}, bf16[128,2048]{1,0:T(8,128)(2,1)S(1)}, u32[]{:S(2)}, u32[]{:S(2)}) collective-permute-start(bf16[128,2048]{1,0:T(8,128)(2,1)} %add.132), channel_id=1, source_target_pairs={{0,1},{1,2},{2,3},{4,5},{5,6},{6,7},{8,9},{9,10},{10,11},{12,13},{... | collective-permute-start | bytes 1572872 | tf_op jit(solution)/shard_map/ppermute | solution.py:585
  175.5 5.6 %collective-permute-start.30 = (f32[2,128]{1,0:T(2,128)S(1)}, f32[2,128]{1,0:T(2,128)S(1)}, u32[]{:S(2)}, u32[]{:S(2)}) collective-permute-start(f32[2,128]{1,0:T(2,128)S(1)} %fusion), channel_id=1, source_target_pairs={{0,3},{1,0},{2,1},{3,2},{4,7},{5,4},{6,5},{7,6},{8,11},{9,8},{10,9... | collective-permute-start | bytes 3080 | tf_op jit(solution)/shard_map/ppermute | solution.py:638
  178.8 4.5 %collective-permute-start.29 = (f32[2,128]{1,0:T(2,128)S(1)}, f32[2,128]{1,0:T(2,128)S(1)}, u32[]{:S(2)}, u32[]{:S(2)}) collective-permute-start(f32[2,128]{1,0:T(2,128)S(1)} %fusion), channel_id=1, source_target_pairs={{0,2},{1,3},{2,0},{3,1},{4,6},{5,7},{6,4},{7,5},{8,10},{9,11},{10,... | collective-permute-start | bytes 3080 | tf_op jit(solution)/shard_map/ppermute | solution.py:638
  179.3 5.4 %collective-permute-start.28 = (f32[2,128]{1,0:T(2,128)S(1)}, f32[2,128]{1,0:T(2,128)S(1)}, u32[]{:S(2)}, u32[]{:S(2)}) collective-permute-start(f32[2,128]{1,0:T(2,128)S(1)} %fusion), channel_id=1, source_target_pairs={{0,1},{1,2},{2,3},{3,0},{4,5},{5,6},{6,7},{7,4},{8,9},{9,10},{10,1... | collective-permute-start | bytes 3080 | tf_op jit(solution)/shard_map/ppermute | solution.py:638
  (20 other events, 298.6 us)
Sparse Core Ops, SparseCore 0:
  61.0 17.1 all-gather.2

commit v3 on v2

--- a/solution.py
+++ b/solution.py
@@ -50,15 +50,13 @@
     return device * heads_dev // (QH // KVH)
 
 
-def prepare_kernel(tp_count, pool_count, heads_dev, hit, lens, place, pool, *refs):
-    counts, needed = refs[:2]
-    sends = refs[2 : 2 + tp_count]
-    own_slots, held, wide, sems = refs[2 + tp_count :]
+def prepare_kernel(tp_count, pool_count, heads_dev, hit, lens, pool, *refs):
+    counts, needed, *sends, own_slots, held, wide, sems = refs
     prompts = counts.shape[0]
     slots_dev, block_rows = pool.shape[:2]
     kv_dev = sends[0].shape[1]
-    pool_index = place[0]
-    tp_index = place[1]
+    pool_index = lax.axis_index("pool")
+    tp_index = lax.axis_index("tp")
     for slot in range(MOST + 1):
         own_slots[slot] = 0
     for prompt in range(prompts):
@@ -100,7 +98,7 @@
                 sends[shift][slot, more] = one_head(head + more, block_rows, wide)
 
 
-def prepare(tp_count, pool_count, heads_dev, kv_dev, hit, lens, place, pool):
+def prepare(tp_count, pool_count, heads_dev, kv_dev, hit, lens, pool):
     prompts = lens.shape[0]
     block_rows = pool.shape[1]
     send = jax.ShapeDtypeStruct((MOST, kv_dev, block_rows, 2 * HD), jnp.bfloat16)
@@ -111,25 +109,25 @@
             jax.ShapeDtypeStruct((tp_count,), jnp.int32),
         ]
         + [send] * tp_count,
-        in_specs=[SMEM(), SMEM(), SMEM(), ANY()],
+        in_specs=[SMEM(), SMEM(), ANY()],
         out_specs=[SMEM()] * 2 + [VMEM()] * tp_count,
         scratch_shapes=[
             pltpu.SMEM((MOST + 1,), jnp.int32),
             pltpu.VMEM((MOST, block_rows, KVH, 2 * HD), jnp.bfloat16),
-            pltpu.VMEM((2, block_rows * KVH, HD), jnp.float32),
+            pltpu.VMEM((2, (block_rows + 1) * KVH, HD), jnp.float32),
             pltpu.SemaphoreType.DMA((MOST,)),
         ],
         compiler_params=pltpu.CompilerParams(vmem_limit_bytes=VMEM_LIMIT),
         cost_estimate=pl.CostEstimate(flops=0, bytes_accessed=8 << 20, transcendentals=0),
         name="prepare",
-    )(hit, lens, place, pool)
+    )(hit, lens, pool)
     return counts, needed, sends
 
 
-def span_kernel(heads_dev, place, span, heads, pieces, wide):
+def span_kernel(heads_dev, span, heads, pieces, wide):
     prompts, rows_dev = span.shape[:2]
     block_rows = pieces.shape[1]
-    tp_index = place[1]
+    tp_index = lax.axis_index("tp")
     for prompt in range(prompts):
         here = pl.ds(pl.multiple_of(tp_index * block_rows, block_rows), block_rows)
         pieces[prompt] = span[prompt, here]
@@ -138,7 +136,7 @@
             heads[more, prompt] = one_head(first_head(tp_index, heads_dev) + more, rows_dev, wide)
 
 
-def span_parts(heads_dev, kv_dev, block_rows, place, span):
+def span_parts(heads_dev, kv_dev, block_rows, span):
     prompts, rows_dev = span.shape[:2]
     return pl.pallas_call(
         functools.partial(span_kernel, heads_dev),
@@ -146,20 +144,20 @@
             jax.ShapeDtypeStruct((kv_dev, prompts, rows_dev, 2 * HD), jnp.bfloat16),
             jax.ShapeDtypeStruct((prompts, block_rows, KVH, 2 * HD), jnp.bfloat16),
         ],
-        in_specs=[SMEM(), VMEM()],
+        in_specs=[VMEM()],
         out_specs=[VMEM()] * 2,
-        scratch_shapes=[pltpu.VMEM((2, rows_dev * KVH, HD), jnp.float32)],
+        scratch_shapes=[pltpu.VMEM((2, (rows_dev + 1) * KVH, HD), jnp.float32)],
         compiler_params=pltpu.CompilerParams(vmem_limit_bytes=VMEM_LIMIT),
         cost_estimate=pl.CostEstimate(flops=0, bytes_accessed=2 << 20, transcendentals=0),
         name="span_parts",
-    )(place, span)
+    )(span)
 
 
 def attend_kernel(
     which_prompts, n_chunks, pool_count, kv_dev, pieces, with_span, with_state, final, block_heads, *refs
 ):
     refs = list(refs)
-    place, lens, counts, query = [refs.pop(0) for _ in range(4)]
+    counts, query = [refs.pop(0) for _ in range(2)]
     chunk_refs = [
         [[refs.pop(0) for _ in range(pool_count)] for _ in range(pieces[chunk])]
         for chunk in range(n_chunks)
@@ -177,7 +175,7 @@
     span_blocks, span_keys, span_valued = [refs.pop(0) for _ in range(3)] if with_span else [None] * 3
     state = refs.pop(0) if with_state else None
     weight = refs.pop(0) if final else None
-    pool_index = place[0]
+    pool_index = lax.axis_index("pool")
     rows_dev = asked_all.shape[1]
     block_rows = blocks.shape[3]
     key_rows = MAXB * block_rows
@@ -193,29 +191,31 @@
         started.append(copy)
         return copy
 
-    brought = []
+    asking = [start(query.at[prompt], asked_all.at[at]) for at, prompt in enumerate(which_prompts)]
+    brought_span, brought = [], []
     for head in range(kv_dev):
         mine = []
-        for at, prompt in enumerate(which_prompts):
-            if head == 0:
-                mine.append(start(query.at[prompt], asked_all.at[at]))
-            if with_span:
+        if with_span:
+            for at, prompt in enumerate(which_prompts):
                 mine += [
                     start(span_refs[r].at[head, prompt], span_blocks.at[head, r, at])
                     for r in range(pool_count)
                 ]
+        if with_state:
+            mine.append(start(state_in.at[head], state.at[head]))
+        brought_span.append(mine)
+        brought.append([])
         for chunk in range(n_chunks):
             split = pieces[chunk] > 1
-            for r in range(pool_count):
-                source = chunk_refs[chunk][head if split else 0][r]
-                mine.append(
+            brought[head].append(
+                [
                     start(
-                        source.at[:, 0 if split else head], blocks.at[head, chunk * pool_count + r]
+                        chunk_refs[chunk][head if split else 0][r].at[:, 0 if split else head],
+                        blocks.at[head, chunk * pool_count + r],
                     )
-                )
-        if with_state:
-            mine.append(start(state_in.at[head], state.at[head]))
-        brought.append(mine)
+                    for r in range(pool_count)
+                ]
+            )
     late = []
     if final:
         width = weight.shape[1]
@@ -231,8 +231,8 @@
             lax.broadcasted_iota(jnp.int32, (rows, 1), 0), rows_dev
         )
 
-    def gather(head, prompt):
-        for chunk in range(n_chunks):
+    def gather(head, prompt, chunk):
+        if chunk is not None:
             offset = jnp.int32(0)
             for r in range(pool_count):
                 first = jnp.int32(0)
@@ -262,7 +262,7 @@
                 return carry
 
             lax.fori_loop(offset, MAXB, fill, 0)
-        if with_span:
+        else:
             for r in range(pool_count):
                 here = pl.ds(r * rows_dev, rows_dev)
                 block = span_blocks[head, r, prompt]
@@ -293,15 +293,21 @@
         return score(head, prompt, first, tiles[at])
 
     for head in range(kv_dev):
-        for copy in brought[head]:
+        for copy in brought_span[head] + (asking if head == 0 else []):
             copy.wait()
+        if with_span:
+            for prompt in range(prompts):
+                gather(head, prompt, None)
+        for chunk in range(n_chunks):
+            for copy in brought[head][chunk]:
+                copy.wait()
+            for prompt in range(prompts):
+                gather(head, prompt, chunk)
         if final and head == 0:
             late = [
                 start(out_w.at[pl.ds(i * part, part), columns], weight.at[pl.ds(i * part, part)])
                 for i in range(WEIGHT_PARTS)
             ]
-        for prompt in range(prompts):
-            gather(head, prompt)
         work = [
             (head, prompt, first, at)
             for prompt in range(prompts)
@@ -361,7 +367,7 @@
 
 
 def attend(
-    which_prompts, place, lens, counts, queries, chunks, kv_dev, span=None, state=None, out_w=None, which=None, width=0
+    which_prompts, counts, queries, chunks, kv_dev, span=None, state=None, out_w=None, which=None, width=0
 ):
     pool_count = len(chunks[0][0])
     n_chunks = len(chunks)
@@ -374,7 +380,7 @@
     block_heads = min(8, group)
     final = out_w is not None
     state_shape = (kv_dev, prompts, group * rows_dev, 2 * HD)
-    operands = [place, lens, counts, queries]
+    operands = [counts, queries]
     operands += [array for chunk in chunks for piece in chunk for array in piece]
     copies = prompts + kv_dev * n_chunks * pool_count
     n_keys = key_rows * n_chunks
@@ -398,7 +404,7 @@
         operands.append(state)
         copies += kv_dev
         later.append(pltpu.VMEM(state_shape, jnp.float32))
-    specs = [SMEM()] * 3 + [ANY()] * (len(operands) - 3)
+    specs = [SMEM()] + [ANY()] * (len(operands) - 1)
     if final:
         operands += [which, out_w]
         specs += [SMEM(), ANY()]
@@ -532,12 +538,11 @@
     kv_dev = max(1, heads_dev // (QH // KVH))
     slots_dev, block_rows = prefix_pool.shape[:2]
     d_dev = residual.shape[2]
-    place = jnp.stack([pool_index, tp_index]).astype(jnp.int32)
 
     counts, needed, sends = prepare(
-        tp_count, pool_count, heads_dev, kv_dev, hit_blocks, prefix_len, place, prefix_pool
+        tp_count, pool_count, heads_dev, kv_dev, hit_blocks, prefix_len, prefix_pool
     )
-    span_own, own_rows = span_parts(heads_dev, kv_dev, block_rows, place, span_kv)
+    span_own, own_rows = span_parts(heads_dev, kv_dev, block_rows, span_kv)
     order = sorted(range(1, tp_count), key=lambda s: -min(s, tp_count - s))
     chunks = [[over_pool(sends[0], pool_count)]]
     span = over_pool(span_own, pool_count)
@@ -556,8 +561,6 @@
     down = tp_index < tp_count // 2
     outs = attend(
         tuple(range(prompts)),
-        place,
-        prefix_len,
         counts,
         queries,
         chunks,

time: 194 us -> 194 us (level)
  local copies, waits for them, and re-layouts: 4.39 us -> 6.33 us
  transfers between devices with their start and end apart: 32 -> 32, of which waited for: 15 -> 15; matrix products, arithmetic and copies ran while one was open for 3% -> 4% of each run, Pallas kernels for 30% -> 29%
where the time goes in v3:
time: 194 us; the launch traced here: 193 us
  Pallas kernels  61.7 us (32%)
  waiting for transfers between devices  58.8 us (30%)
  starting transfers between devices  44.3 us (23%)
  between operations  14.4 us (7%)
  other arithmetic  7.63 us (4%)
  local copies, waits for them, and re-layouts  6.33 us (3%)
    ppermute x5, waiting for transfers between devices, over_pool(): arrived = array if chips == 0 else lax.ppermute(array, 'pool', pairs)  34.4 us
    pallas_call x1, Pallas kernels, attend(): pl.pallas_call(functools.partial(attend_kernel, which_prompts, n_chunks,...  26.5 us
    ppermute x4, starting transfers between devices, send(): lax.ppermute(to_right, 'tp', right)  16.4 us
    pallas_call x1, Pallas kernels, project(): pl.pallas_call(project_kernel, grid_spec=pltpu.PrefetchScalarGridSpec(num...  14.4 us
    pallas_call x6, Pallas kernels, add(): pl.pallas_call(functools.partial(add_kernel, int(begun is not None)), gri...  13.6 us
    ppermute x4, waiting for transfers between devices, send(): lax.ppermute(to_left, 'tp', left)  6.75 us
    ppermute x3, starting transfers between devices, local(): along = lax.ppermute(block, 'tp', pairs)  6.62 us
    ppermute x3, waiting for transfers between devices, local(): along = lax.ppermute(block, 'tp', pairs)  5.71 us
  transfers between devices with their start and end apart: 32, of which 15 were waited for; matrix products, arithmetic and copies ran while one was open for 4% of the time, Pallas kernels for 29%

profile of v3, /device:TPU:0, one launch (start us, length us, event | category | flops | bytes accessed | tf_op | source)
XLA Modules:
  0.0 193.0 jit_solution(4211159155060451541)
XLA Ops:
  7.2 5.0 %prepare.1 = (s32[2,4]{1,0:T(2,128)}, s32[4]{0:T(128)}, bf16[12,2,32,256]{3,2,1,0:T(8,128)(2,1)}, bf16[12,2,32,256]{3,2,1,0:T(8,128)(2,1)}, bf16[12,2,32,256]{3,...) custom-call(s32[2,24]{1,0:T(2,128)} %hit.1, s32[2]{0:T(128)} %lens.1, bf16[24,32,8,256]{3,2,1,0:T(8,128)(2,1)} %pool.1), custom_call_target="tpu_custom_call" | custom-call | bytes 8388608 | tf_op jit(solution)/shard_map/prepare/pallas_call | solution.py:105
  12.2 4.1 %collective-permute-start.3 = (bf16[12,2,32,256]{3,2,1,0:T(8,128)(2,1)}, bf16[12,2,32,256]{3,2,1,0:T(8,128)(2,1)S(1)}, u32[]{:S(2)}, u32[]{:S(2)}) collective-permute-start(bf16[12,2,32,256]{3,2,1,0:T(8,128)(2,1)} %get-tuple-element.26), channel_id=1, source_target_pairs={{0,2},{1,3},{2,0},{3,1},{4,6},{5,7},{6,4},{7,5},{8,10},{9,11},{10,... | collective-permute-start | bytes 1179656 | tf_op jit(solution)/shard_map/ppermute | solution.py:555
  17.8 2.2 %span_parts.1 = (bf16[2,2,128,256]{3,2,1,0:T(8,128)(2,1)}, bf16[2,32,8,256]{3,2,1,0:T(8,128)(2,1)}) custom-call(bf16[2,128,8,256]{3,2,1,0:T(8,128)(2,1)} %span.1), custom_call_target="tpu_custom_call" | custom-call | bytes 2097152 | tf_op jit(solution)/shard_map/span_parts/pallas_call | solution.py:141
  20.6 12.3 %collective-permute-done.4.refs_20_ = bf16[2,2,128,256]{3,2,1,0:T(8,128)(2,1)} collective-permute-done((bf16[2,2,128,256]{3,2,1,0:T(8,128)(2,1)}, bf16[2,2,128,256]{3,2,1,0:T(8,128)(2,1)}, u32[]{:S(2)}, u32[]{:S(2)}) %collective-permute-start.4) | collective-permute-done | bytes 262176 | tf_op jit(solution)/shard_map/ppermute | solution.py:521
  34.1 1.5 collective-permute-start.6
  36.4 8.0 %collective-permute-done.6.refs_8_ = bf16[12,2,32,256]{3,2,1,0:T(8,128)(2,1)S(1)} collective-permute-done((bf16[12,2,32,256]{3,2,1,0:T(8,128)(2,1)S(1)}, bf16[12,2,32,256]{3,2,1,0:T(8,128)(2,1)S(1)}, u32[]{:S(2)}, u32[]{:S(2)}) %collective-permute-start.6) | collective-permute-done | bytes 393248 | tf_op jit(solution)/shard_map/ppermute | solution.py:521
  44.4 4.0 %collective-permute-done.8.refs_10_ = bf16[12,2,32,256]{3,2,1,0:T(8,128)(2,1)S(1)} collective-permute-done((bf16[12,2,32,256]{3,2,1,0:T(8,128)(2,1)}, bf16[12,2,32,256]{3,2,1,0:T(8,128)(2,1)S(1)}, u32[]{:S(2)}, u32[]{:S(2)}) %collective-permute-start.8) | collective-permute-done | bytes 393248 | tf_op jit(solution)/shard_map/ppermute | solution.py:555
  48.9 1.7 collective-permute-start.12
  51.1 7.0 %collective-permute-done.10.refs_12_ = bf16[12,2,32,256]{3,2,1,0:T(8,128)(2,1)S(1)} collective-permute-done((bf16[12,2,32,256]{3,2,1,0:T(8,128)(2,1)S(1)}, bf16[12,2,32,256]{3,2,1,0:T(8,128)(2,1)S(1)}, u32[]{:S(2)}, u32[]{:S(2)}) %collective-permute-start.10) | collective-permute-done | bytes 393248 | tf_op jit(solution)/shard_map/ppermute | solution.py:521
  62.6 7.1 %collective-permute-done.14.refs_16_ = bf16[12,2,32,256]{3,2,1,0:T(8,128)(2,1)} collective-permute-done((bf16[12,2,32,256]{3,2,1,0:T(8,128)(2,1)S(1)}, bf16[12,2,32,256]{3,2,1,0:T(8,128)(2,1)}, u32[]{:S(2)}, u32[]{:S(2)}) %collective-permute-start.14) | collective-permute-done | bytes 393248 | tf_op jit(solution)/shard_map/ppermute | solution.py:521
  69.9 1.8 collective-permute-done.15.refs_17_
  72.5 26.5 %attend.1 = (bf16[128,2048]{1,0:T(8,128)(2,1)}, bf16[128,2048]{1,0:T(8,128)(2,1)}, bf16[128,2048]{1,0:T(8,128)(2,1)}, bf16[128,2048]{1,0:T(8,128)(2,1)}) custom-call(s32[2,4]{1,0:T(2,128)} %get-tuple-element.24.refs_0_, bf16[2,128,2048]{2,1,0:T(8,128)(2,1)} %refs_1_.1, bf16[12,2,32,256]{3,2,1,0:T(8,128)(2,1)} %get-tuple-element.25.refs_2_, ...), custom_call_target="tpu_custom_call" | custom-call | flops 13421772800 | bytes 16777216 | tf_op jit(solution)/shard_map/attend/pallas_call | solution.py:418
  101.6 14.4 %project.1.partial = bf16[3,256,2048]{2,1,0:T(8,128)(2,1)} custom-call(s32[4]{0:T(128)} %get-tuple-element.23.refs_22_.which, bf16[128,2048]{1,0:T(8,128)(2,1)} %get-tuple-element.35.refs_0_, bf16[128,2048]{1,0:T(8,128)(2,1)} %get-tuple-element.36.refs_1_, bf16[2048,8192]{1,0:T(8,128)(2,1)} %refs_2_.1), custom_call_target="tpu_custom_call" | custom-call | flops 6442450944 | bytes 31457280 | tf_op jit(solution)/shard_map/project/pallas_call | solution.py:457
  116.9 2.1 %add.126 = bf16[128,2048]{1,0:T(8,128)(2,1)} custom-call(s32[1]{0:T(128)} %constant.11.clone.1.which, bf16[3,256,2048]{2,1,0:T(8,128)(2,1)} %project.1.partial, bf16[128,2048]{1,0:T(8,128)(2,1)} %copy-done.4), custom_call_target="tpu_custom_call" | custom-call | flops 262144 | bytes 2097152 | tf_op jit(solution)/shard_map/add/pallas_call | solution.py:494
  119.0 2.1 %collective-permute-start.19 = (bf16[128,2048]{1,0:T(8,128)(2,1)}, bf16[128,2048]{1,0:T(8,128)(2,1)}, u32[]{:S(2)}, u32[]{:S(2)}) collective-permute-start(bf16[128,2048]{1,0:T(8,128)(2,1)} %add.126), channel_id=1, source_target_pairs={{0,1},{1,2},{4,5},{5,6},{8,9},{9,10},{12,13},{13,14},{16,17},{17,1... | collective-permute-start | bytes 1572872 | tf_op jit(solution)/shard_map/ppermute | solution.py:588
  122.6 1.5 collective-permute-done.23.refs_0_
  124.9 2.1 %add.129 = bf16[128,2048]{1,0:T(8,128)(2,1)} custom-call(s32[1]{0:T(128)} %constant.11.clone.1.which, bf16[3,256,2048]{2,1,0:T(8,128)(2,1)} %project.1.partial, bf16[128,2048]{1,0:T(8,128)(2,1)} %copy-done.3), custom_call_target="tpu_custom_call" | custom-call | flops 262144 | bytes 2097152 | tf_op jit(solution)/shard_map/add/pallas_call | solution.py:494
  128.4 4.9 %collective-permute-start.24 = (bf16[128,2048]{1,0:T(8,128)(2,1)}, bf16[128,2048]{1,0:T(8,128)(2,1)}, u32[]{:S(2)}, u32[]{:S(2)}) collective-permute-start(bf16[128,2048]{1,0:T(8,128)(2,1)} %add.129), channel_id=1, source_target_pairs={{0,1},{1,2},{4,5},{5,6},{8,9},{9,10},{12,13},{13,14},{16,17},{17,1... | collective-permute-start | bytes 1572872 | tf_op jit(solution)/shard_map/ppermute | solution.py:588
  133.4 3.9 %gather_fusion = bf16[24,32,8,256]{3,2,1,0:T(8,128)(2,1)} fusion(bf16[8,32,8,256]{3,2,1,0:T(8,128)(2,1)} %bitcast.27, s32[1024]{0:T(1024)S(1)} %pad_clamp_fusion), kind=kCustom, calls=%fused_computation | custom fusion | bytes 6291552 | tf_op jit(solution)/shard_map/jit(_take)/gather | solution.py:598
  137.3 4.0 %select_select_fusion = bf16[24,32,8,256]{3,2,1,0:T(8,128)(2,1)} fusion(bf16[24,32,8,256]{3,2,1,0:T(8,128)(2,1)S(1)} %copy-done, bf16[24,32,8,256]{3,2,1,0:T(8,128)(2,1)} %gather_fusion, pred[24]{0:T(512)(128)(4,1)S(1)} %get-tuple-element.47, pred[24]{0:T(512)(128)(4,1)S(1)} %get-tuple-element.48), kind=kLoop, calls=%fused_computation.1 | loop fusion | flops 3145728 | bytes 9437232 | tf_op jit(solution)/shard_map/jit(_where)/select_n | solution.py:597
  141.2 2.3 %add.128 = bf16[128,2048]{1,0:T(8,128)(2,1)} custom-call(s32[1]{0:T(128)} %bitcast.5.which, bf16[3,256,2048]{2,1,0:T(8,128)(2,1)} %project.1.partial, bf16[128,2048]{1,0:T(8,128)(2,1)} %get-tuple-element.37.refs_0_, bf16[128,2048]{1,0:T(8,128)(2,1)} %collective-permute-done.20.refs_1_), custom_call_target="tpu_custom_call" | custom-call | flops 262144 | bytes 2097152 | tf_op jit(solution)/shard_map/add/pallas_call | solution.py:494
  144.9 2.3 %add.127 = bf16[128,2048]{1,0:T(8,128)(2,1)} custom-call(s32[1]{0:T(128)} %bitcast.1.which, bf16[3,256,2048]{2,1,0:T(8,128)(2,1)} %project.1.partial, bf16[128,2048]{1,0:T(8,128)(2,1)} %get-tuple-element.37.refs_0_, bf16[128,2048]{1,0:T(8,128)(2,1)} %collective-permute-done.19.refs_1_), custom_call_target="tpu_custom_call" | custom-call | flops 262144 | bytes 2097152 | tf_op jit(solution)/shard_map/add/pallas_call | solution.py:494
  147.2 4.7 %collective-permute-start.21 = (bf16[128,2048]{1,0:T(8,128)(2,1)}, bf16[128,2048]{1,0:T(8,128)(2,1)S(1)}, u32[]{:S(2)}, u32[]{:S(2)}) collective-permute-start(bf16[128,2048]{1,0:T(8,128)(2,1)} %add.127), channel_id=1, source_target_pairs={{0,1},{1,2},{2,3},{4,5},{5,6},{6,7},{8,9},{9,10},{10,11},{12,13},{... | collective-permute-start | bytes 1572872 | tf_op jit(solution)/shard_map/ppermute | solution.py:588
  151.9 2.4 %add.131 = bf16[128,2048]{1,0:T(8,128)(2,1)} custom-call(s32[1]{0:T(128)} %bitcast.5.which, bf16[3,256,2048]{2,1,0:T(8,128)(2,1)} %project.1.partial, bf16[128,2048]{1,0:T(8,128)(2,1)} %get-tuple-element.41.refs_0_, bf16[128,2048]{1,0:T(8,128)(2,1)} %collective-permute-done.26.refs_1_), custom_call_target="tpu_custom_call" | custom-call | flops 262144 | bytes 2097152 | tf_op jit(solution)/shard_map/add/pallas_call | solution.py:494
  155.7 2.3 %add.130 = bf16[128,2048]{1,0:T(8,128)(2,1)} custom-call(s32[1]{0:T(128)} %bitcast.1.which, bf16[3,256,2048]{2,1,0:T(8,128)(2,1)} %project.1.partial, bf16[128,2048]{1,0:T(8,128)(2,1)} %get-tuple-element.41.refs_0_, bf16[128,2048]{1,0:T(8,128)(2,1)} %collective-permute-done.24.refs_1_), custom_call_target="tpu_custom_call" | custom-call | flops 262144 | bytes 2097152 | tf_op jit(solution)/shard_map/add/pallas_call | solution.py:494
  158.1 4.7 %collective-permute-start.25 = (bf16[128,2048]{1,0:T(8,128)(2,1)}, bf16[128,2048]{1,0:T(8,128)(2,1)S(1)}, u32[]{:S(2)}, u32[]{:S(2)}) collective-permute-start(bf16[128,2048]{1,0:T(8,128)(2,1)} %add.130), channel_id=1, source_target_pairs={{0,1},{1,2},{2,3},{4,5},{5,6},{6,7},{8,9},{9,10},{10,11},{12,13},{... | collective-permute-start | bytes 1572872 | tf_op jit(solution)/shard_map/ppermute | solution.py:588
  163.0 6.7 %collective-permute-done.27 = bf16[128,2048]{1,0:T(8,128)(2,1)S(1)} collective-permute-done((bf16[128,2048]{1,0:T(8,128)(2,1)}, bf16[128,2048]{1,0:T(8,128)(2,1)S(1)}, u32[]{:S(2)}, u32[]{:S(2)}) %collective-permute-start.27) | collective-permute-done | bytes 524320 | tf_op jit(solution)/shard_map/ppermute | solution.py:588
  169.7 3.6 %collective-permute-done.25 = bf16[128,2048]{1,0:T(8,128)(2,1)S(1)} collective-permute-done((bf16[128,2048]{1,0:T(8,128)(2,1)}, bf16[128,2048]{1,0:T(8,128)(2,1)S(1)}, u32[]{:S(2)}, u32[]{:S(2)}) %collective-permute-start.25) | collective-permute-done | bytes 524320 | tf_op jit(solution)/shard_map/ppermute | solution.py:588
  173.3 1.9 fusion.7
  175.6 3.3 %collective-permute-start.30 = (f32[2,128]{1,0:T(2,128)S(1)}, f32[2,128]{1,0:T(2,128)S(1)}, u32[]{:S(2)}, u32[]{:S(2)}) collective-permute-start(f32[2,128]{1,0:T(2,128)S(1)} %fusion), channel_id=1, source_target_pairs={{0,3},{1,0},{2,1},{3,2},{4,7},{5,4},{6,5},{7,6},{8,11},{9,8},{10,9... | collective-permute-start | bytes 3080 | tf_op jit(solution)/shard_map/ppermute | solution.py:641
  179.5 1.7 collective-permute-start.28
  181.3 2.2 %collective-permute-done.29 = f32[2,128]{1,0:T(2,128)S(1)} collective-permute-done((f32[2,128]{1,0:T(2,128)S(1)}, f32[2,128]{1,0:T(2,128)S(1)}, u32[]{:S(2)}, u32[]{:S(2)}) %collective-permute-start.29) | collective-permute-done | bytes 1056 | tf_op jit(solution)/shard_map/ppermute | solution.py:641
  (99 shorter events, 24.2 us)
Async XLA Ops:
  7.2 126.2 %all-gather.3.cloned.1.call-start = ((), (), s32[]{:S(2)}) async-start(), calls=%async_computation | async-start | bytes 1310720 | tf_op jit(solution)/shard_map/all_gather | solution.py:590
  12.2 21.9 %collective-permute-start.3 = (bf16[12,2,32,256]{3,2,1,0:T(8,128)(2,1)}, bf16[12,2,32,256]{3,2,1,0:T(8,128)(2,1)S(1)}, u32[]{:S(2)}, u32[]{:S(2)}) collective-permute-start(bf16[12,2,32,256]{3,2,1,0:T(8,128)(2,1)} %get-tuple-element.26), channel_id=1, source_target_pairs={{0,2},{1,3},{2,0},{3,1},{4,6},{5,7},{6,4},{7,5},{8,10},{9,11},{10,... | collective-permute-start | bytes 1179656 | tf_op jit(solution)/shard_map/ppermute | solution.py:555
  16.3 19.3 %collective-permute-start.1 = (bf16[12,2,32,256]{3,2,1,0:T(8,128)(2,1)}, bf16[12,2,32,256]{3,2,1,0:T(8,128)(2,1)S(1)}, u32[]{:S(2)}, u32[]{:S(2)}) collective-permute-start(bf16[12,2,32,256]{3,2,1,0:T(8,128)(2,1)} %get-tuple-element.25.refs_2_), channel_id=1, source_target_pairs={{0,8},{4,12},{8,0},{12,4},{1,9},{5,13},{9,1},{13,5},{2,10},{6,14},... | collective-permute-start | bytes 1179656 | tf_op jit(solution)/shard_map/ppermute | solution.py:521
  20.0 12.8 %collective-permute-start.4 = (bf16[2,2,128,256]{3,2,1,0:T(8,128)(2,1)}, bf16[2,2,128,256]{3,2,1,0:T(8,128)(2,1)}, u32[]{:S(2)}, u32[]{:S(2)}) collective-permute-start(bf16[2,2,128,256]{3,2,1,0:T(8,128)(2,1)} %get-tuple-element.27.refs_18_), channel_id=1, source_target_pairs={{0,8},{4,12},{8,0},{12,4},{1,9},{5,13},{9,1},{13,5},{2,10},{6,14},... | collective-permute-start | bytes 786440 | tf_op jit(solution)/shard_map/ppermute | solution.py:521
  34.1 10.3 %collective-permute-start.6 = (bf16[12,2,32,256]{3,2,1,0:T(8,128)(2,1)S(1)}, bf16[12,2,32,256]{3,2,1,0:T(8,128)(2,1)S(1)}, u32[]{:S(2)}, u32[]{:S(2)}) collective-permute-start(bf16[12,2,32,256]{3,2,1,0:T(8,128)(2,1)S(1)} %collective-permute-done.3.refs_6_), channel_id=1, source_target_pairs={{0,8},{4,12},{8,0},{12,4},{1,9},{5,13},{9,1},{13,5},{2,10},{6,14},... | collective-permute-start | bytes 1179656 | tf_op jit(solution)/shard_map/ppermute | solution.py:521
  35.6 12.7 %collective-permute-start.8 = (bf16[12,2,32,256]{3,2,1,0:T(8,128)(2,1)}, bf16[12,2,32,256]{3,2,1,0:T(8,128)(2,1)S(1)}, u32[]{:S(2)}, u32[]{:S(2)}) collective-permute-start(bf16[12,2,32,256]{3,2,1,0:T(8,128)(2,1)} %get-tuple-element.30), channel_id=1, source_target_pairs={{0,1},{1,2},{2,3},{3,0},{4,5},{5,6},{6,7},{7,4},{8,9},{9,10},{10,1... | collective-permute-start | bytes 1179656 | tf_op jit(solution)/shard_map/ppermute | solution.py:555
  48.3 9.8 %collective-permute-start.10 = (bf16[12,2,32,256]{3,2,1,0:T(8,128)(2,1)S(1)}, bf16[12,2,32,256]{3,2,1,0:T(8,128)(2,1)S(1)}, u32[]{:S(2)}, u32[]{:S(2)}) collective-permute-start(bf16[12,2,32,256]{3,2,1,0:T(8,128)(2,1)S(1)} %collective-permute-done.8.refs_10_), channel_id=1, source_target_pairs={{0,8},{4,12},{8,0},{12,4},{1,9},{5,13},{9,1},{13,5},{2,10},{6,14},... | collective-permute-start | bytes 1179656 | tf_op jit(solution)/shard_map/ppermute | solution.py:521
  48.9 9.8 %collective-permute-start.12 = (bf16[12,2,32,256]{3,2,1,0:T(8,128)(2,1)}, bf16[12,2,32,256]{3,2,1,0:T(8,128)(2,1)S(1)}, u32[]{:S(2)}, u32[]{:S(2)}) collective-permute-start(bf16[12,2,32,256]{3,2,1,0:T(8,128)(2,1)} %get-tuple-element.33), channel_id=1, source_target_pairs={{0,3},{1,0},{2,1},{3,2},{4,7},{5,4},{6,5},{7,6},{8,11},{9,8},{10,9... | collective-permute-start | bytes 1179656 | tf_op jit(solution)/shard_map/ppermute | solution.py:555
  50.6 9.5 %collective-permute-start.16 = (bf16[2,2,128,256]{3,2,1,0:T(8,128)(2,1)}, bf16[2,2,128,256]{3,2,1,0:T(8,128)(2,1)}, u32[]{:S(2)}, u32[]{:S(2)}) collective-permute-start(bf16[2,2,128,256]{3,2,1,0:T(8,128)(2,1)} %get-tuple-element.27.refs_18_), channel_id=1, source_target_pairs={{0,4},{4,0},{8,12},{12,8},{1,5},{5,1},{9,13},{13,9},{2,6},{6,2},{1... | collective-permute-start | bytes 786440 | tf_op jit(solution)/shard_map/ppermute | solution.py:525
  50.6 9.7 %collective-permute-start = (bf16[12,2,32,256]{3,2,1,0:T(8,128)(2,1)}, bf16[12,2,32,256]{3,2,1,0:T(8,128)(2,1)S(1)}, u32[]{:S(2)}, u32[]{:S(2)}) collective-permute-start(bf16[12,2,32,256]{3,2,1,0:T(8,128)(2,1)} %get-tuple-element.25.refs_2_), channel_id=1, source_target_pairs={{0,4},{4,0},{8,12},{12,8},{1,5},{5,1},{9,13},{13,9},{2,6},{6,2},{1... | collective-permute-start | bytes 1179656 | tf_op jit(solution)/shard_map/ppermute | solution.py:525
  51.1 11.4 %collective-permute-start.5 = (bf16[12,2,32,256]{3,2,1,0:T(8,128)(2,1)S(1)}, bf16[12,2,32,256]{3,2,1,0:T(8,128)(2,1)S(1)}, u32[]{:S(2)}, u32[]{:S(2)}) collective-permute-start(bf16[12,2,32,256]{3,2,1,0:T(8,128)(2,1)S(1)} %collective-permute-done.3.refs_6_), channel_id=1, source_target_pairs={{0,4},{4,0},{8,12},{12,8},{1,5},{5,1},{9,13},{13,9},{2,6},{6,2},{1... | collective-permute-start | bytes 1179656 | tf_op jit(solution)/shard_map/ppermute | solution.py:525
  58.1 4.0 %collective-permute-start.2 = (bf16[12,2,32,256]{3,2,1,0:T(8,128)(2,1)S(1)}, bf16[12,2,32,256]{3,2,1,0:T(8,128)(2,1)S(1)}, u32[]{:S(2)}, u32[]{:S(2)}) collective-permute-start(bf16[12,2,32,256]{3,2,1,0:T(8,128)(2,1)S(1)} %collective-permute-done.1.refs_4_), channel_id=1, source_target_pairs={{0,4},{4,0},{8,12},{12,8},{1,5},{5,1},{9,13},{13,9},{2,6},{6,2},{1... | collective-permute-start | bytes 1179656 | tf_op jit(solution)/shard_map/ppermute | solution.py:525
  58.6 11.1 %collective-permute-start.14 = (bf16[12,2,32,256]{3,2,1,0:T(8,128)(2,1)S(1)}, bf16[12,2,32,256]{3,2,1,0:T(8,128)(2,1)}, u32[]{:S(2)}, u32[]{:S(2)}) collective-permute-start(bf16[12,2,32,256]{3,2,1,0:T(8,128)(2,1)S(1)} %collective-permute-done.12.refs_14_), channel_id=1, source_target_pairs={{0,8},{4,12},{8,0},{12,4},{1,9},{5,13},{9,1},{13,5},{2,10},{6,14},... | collective-permute-start | bytes 1179656 | tf_op jit(solution)/shard_map/ppermute | solution.py:521
  60.1 1.9 collective-permute-start.17
  60.3 9.5 %collective-permute-start.9 = (bf16[12,2,32,256]{3,2,1,0:T(8,128)(2,1)S(1)}, bf16[12,2,32,256]{3,2,1,0:T(8,128)(2,1)S(1)}, u32[]{:S(2)}, u32[]{:S(2)}) collective-permute-start(bf16[12,2,32,256]{3,2,1,0:T(8,128)(2,1)S(1)} %collective-permute-done.8.refs_10_), channel_id=1, source_target_pairs={{0,4},{4,0},{8,12},{12,8},{1,5},{5,1},{9,13},{13,9},{2,6},{6,2},{1... | collective-permute-start | bytes 1179656 | tf_op jit(solution)/shard_map/ppermute | solution.py:525
  62.0 7.8 %collective-permute-start.7 = (bf16[12,2,32,256]{3,2,1,0:T(8,128)(2,1)S(1)}, bf16[12,2,32,256]{3,2,1,0:T(8,128)(2,1)S(1)}, u32[]{:S(2)}, u32[]{:S(2)}) collective-permute-start(bf16[12,2,32,256]{3,2,1,0:T(8,128)(2,1)S(1)} %collective-permute-done.6.refs_8_), channel_id=1, source_target_pairs={{0,4},{4,0},{8,12},{12,8},{1,5},{5,1},{9,13},{13,9},{2,6},{6,2},{1... | collective-permute-start | bytes 1179656 | tf_op jit(solution)/shard_map/ppermute | solution.py:525
  62.1 7.7 %collective-permute-start.13 = (bf16[12,2,32,256]{3,2,1,0:T(8,128)(2,1)S(1)}, bf16[12,2,32,256]{3,2,1,0:T(8,128)(2,1)S(1)}, u32[]{:S(2)}, u32[]{:S(2)}) collective-permute-start(bf16[12,2,32,256]{3,2,1,0:T(8,128)(2,1)S(1)} %collective-permute-done.12.refs_14_), channel_id=1, source_target_pairs={{0,4},{4,0},{8,12},{12,8},{1,5},{5,1},{9,13},{13,9},{2,6},{6,2},{1... | collective-permute-start | bytes 1179656 | tf_op jit(solution)/shard_map/ppermute | solution.py:525
  62.5 7.3 %collective-permute-start.11 = (bf16[12,2,32,256]{3,2,1,0:T(8,128)(2,1)S(1)}, bf16[12,2,32,256]{3,2,1,0:T(8,128)(2,1)S(1)}, u32[]{:S(2)}, u32[]{:S(2)}) collective-permute-start(bf16[12,2,32,256]{3,2,1,0:T(8,128)(2,1)S(1)} %collective-permute-done.10.refs_12_), channel_id=1, source_target_pairs={{0,4},{4,0},{8,12},{12,8},{1,5},{5,1},{9,13},{13,9},{2,6},{6,2},{1... | collective-permute-start | bytes 1179656 | tf_op jit(solution)/shard_map/ppermute | solution.py:525
  69.8 1.9 %collective-permute-start.15 = (bf16[12,2,32,256]{3,2,1,0:T(8,128)(2,1)}, bf16[12,2,32,256]{3,2,1,0:T(8,128)(2,1)S(1)}, u32[]{:S(2)}, u32[]{:S(2)}) collective-permute-start(bf16[12,2,32,256]{3,2,1,0:T(8,128)(2,1)} %collective-permute-done.14.refs_16_), channel_id=1, source_target_pairs={{0,4},{4,0},{8,12},{12,8},{1,5},{5,1},{9,13},{13,9},{2,6},{6,2},{1... | collective-permute-start | bytes 1179656 | tf_op jit(solution)/shard_map/ppermute | solution.py:525
  99.0 17.1 %collective-permute-start.18 = (bf16[128,2048]{1,0:T(8,128)(2,1)}, bf16[128,2048]{1,0:T(8,128)(2,1)S(1)}, u32[]{:S(2)}, u32[]{:S(2)}) collective-permute-start(bf16[128,2048]{1,0:T(8,128)(2,1)} %get-tuple-element.37.refs_0_), channel_id=1, source_target_pairs={{0,1},{3,2},{4,5},{7,6},{8,9},{11,10},{12,13},{15,14},{16,17},{19,... | collective-permute-start | bytes 1572872 | tf_op jit(solution)/shard_map/ppermute | solution.py:587
  100.3 23.8 %collective-permute-start.23 = (bf16[128,2048]{1,0:T(8,128)(2,1)}, bf16[128,2048]{1,0:T(8,128)(2,1)S(1)}, u32[]{:S(2)}, u32[]{:S(2)}) collective-permute-start(bf16[128,2048]{1,0:T(8,128)(2,1)} %get-tuple-element.41.refs_0_), channel_id=1, source_target_pairs={{0,1},{3,2},{4,5},{7,6},{8,9},{11,10},{12,13},{15,14},{16,17},{19,... | collective-permute-start | bytes 1572872 | tf_op jit(solution)/shard_map/ppermute | solution.py:587
  119.0 22.3 %collective-permute-start.19 = (bf16[128,2048]{1,0:T(8,128)(2,1)}, bf16[128,2048]{1,0:T(8,128)(2,1)}, u32[]{:S(2)}, u32[]{:S(2)}) collective-permute-start(bf16[128,2048]{1,0:T(8,128)(2,1)} %add.126), channel_id=1, source_target_pairs={{0,1},{1,2},{4,5},{5,6},{8,9},{9,10},{12,13},{13,14},{16,17},{17,1... | collective-permute-start | bytes 1572872 | tf_op jit(solution)/shard_map/ppermute | solution.py:588
  121.1 20.2 %collective-permute-start.20 = (bf16[128,2048]{1,0:T(8,128)(2,1)}, bf16[128,2048]{1,0:T(8,128)(2,1)}, u32[]{:S(2)}, u32[]{:S(2)}) collective-permute-start(bf16[128,2048]{1,0:T(8,128)(2,1)} %add.126), channel_id=1, source_target_pairs={{2,1},{3,2},{6,5},{7,6},{10,9},{11,10},{14,13},{15,14},{18,17},{19... | collective-permute-start | bytes 1572872 | tf_op jit(solution)/shard_map/ppermute | solution.py:588
  127.0 25.0 %collective-permute-start.26 = (bf16[128,2048]{1,0:T(8,128)(2,1)}, bf16[128,2048]{1,0:T(8,128)(2,1)}, u32[]{:S(2)}, u32[]{:S(2)}) collective-permute-start(bf16[128,2048]{1,0:T(8,128)(2,1)} %add.129), channel_id=1, source_target_pairs={{2,1},{3,2},{6,5},{7,6},{10,9},{11,10},{14,13},{15,14},{18,17},{19... | collective-permute-start | bytes 1572872 | tf_op jit(solution)/shard_map/ppermute | solution.py:588
  128.4 27.3 %collective-permute-start.24 = (bf16[128,2048]{1,0:T(8,128)(2,1)}, bf16[128,2048]{1,0:T(8,128)(2,1)}, u32[]{:S(2)}, u32[]{:S(2)}) collective-permute-start(bf16[128,2048]{1,0:T(8,128)(2,1)} %add.129), channel_id=1, source_target_pairs={{0,1},{1,2},{4,5},{5,6},{8,9},{9,10},{12,13},{13,14},{16,17},{17,1... | collective-permute-start | bytes 1572872 | tf_op jit(solution)/shard_map/ppermute | solution.py:588
  143.6 19.2 %collective-permute-start.22 = (bf16[128,2048]{1,0:T(8,128)(2,1)}, bf16[128,2048]{1,0:T(8,128)(2,1)S(1)}, u32[]{:S(2)}, u32[]{:S(2)}) collective-permute-start(bf16[128,2048]{1,0:T(8,128)(2,1)} %add.128), channel_id=1, source_target_pairs={{1,0},{2,1},{3,2},{5,4},{6,5},{7,6},{9,8},{10,9},{11,10},{13,12},{... | collective-permute-start | bytes 1572872 | tf_op jit(solution)/shard_map/ppermute | solution.py:588
  147.2 15.8 %collective-permute-start.21 = (bf16[128,2048]{1,0:T(8,128)(2,1)}, bf16[128,2048]{1,0:T(8,128)(2,1)S(1)}, u32[]{:S(2)}, u32[]{:S(2)}) collective-permute-start(bf16[128,2048]{1,0:T(8,128)(2,1)} %add.127), channel_id=1, source_target_pairs={{0,1},{1,2},{2,3},{4,5},{5,6},{6,7},{8,9},{9,10},{10,11},{12,13},{... | collective-permute-start | bytes 1572872 | tf_op jit(solution)/shard_map/ppermute | solution.py:588
  154.3 15.4 %collective-permute-start.27 = (bf16[128,2048]{1,0:T(8,128)(2,1)}, bf16[128,2048]{1,0:T(8,128)(2,1)S(1)}, u32[]{:S(2)}, u32[]{:S(2)}) collective-permute-start(bf16[128,2048]{1,0:T(8,128)(2,1)} %add.131), channel_id=1, source_target_pairs={{1,0},{2,1},{3,2},{5,4},{6,5},{7,6},{9,8},{10,9},{11,10},{13,12},{... | collective-permute-start | bytes 1572872 | tf_op jit(solution)/shard_map/ppermute | solution.py:588
  158.1 15.3 %collective-permute-start.25 = (bf16[128,2048]{1,0:T(8,128)(2,1)}, bf16[128,2048]{1,0:T(8,128)(2,1)S(1)}, u32[]{:S(2)}, u32[]{:S(2)}) collective-permute-start(bf16[128,2048]{1,0:T(8,128)(2,1)} %add.130), channel_id=1, source_target_pairs={{0,1},{1,2},{2,3},{4,5},{5,6},{6,7},{8,9},{9,10},{10,11},{12,13},{... | collective-permute-start | bytes 1572872 | tf_op jit(solution)/shard_map/ppermute | solution.py:588
  175.6 5.6 %collective-permute-start.30 = (f32[2,128]{1,0:T(2,128)S(1)}, f32[2,128]{1,0:T(2,128)S(1)}, u32[]{:S(2)}, u32[]{:S(2)}) collective-permute-start(f32[2,128]{1,0:T(2,128)S(1)} %fusion), channel_id=1, source_target_pairs={{0,3},{1,0},{2,1},{3,2},{4,7},{5,4},{6,5},{7,6},{8,11},{9,8},{10,9... | collective-permute-start | bytes 3080 | tf_op jit(solution)/shard_map/ppermute | solution.py:641
  179.0 4.5 %collective-permute-start.29 = (f32[2,128]{1,0:T(2,128)S(1)}, f32[2,128]{1,0:T(2,128)S(1)}, u32[]{:S(2)}, u32[]{:S(2)}) collective-permute-start(f32[2,128]{1,0:T(2,128)S(1)} %fusion), channel_id=1, source_target_pairs={{0,2},{1,3},{2,0},{3,1},{4,6},{5,7},{6,4},{7,5},{8,10},{9,11},{10,... | collective-permute-start | bytes 3080 | tf_op jit(solution)/shard_map/ppermute | solution.py:641
  179.5 5.4 %collective-permute-start.28 = (f32[2,128]{1,0:T(2,128)S(1)}, f32[2,128]{1,0:T(2,128)S(1)}, u32[]{:S(2)}, u32[]{:S(2)}) collective-permute-start(f32[2,128]{1,0:T(2,128)S(1)} %fusion), channel_id=1, source_target_pairs={{0,1},{1,2},{2,3},{3,0},{4,5},{5,6},{6,7},{7,4},{8,9},{9,10},{10,1... | collective-permute-start | bytes 3080 | tf_op jit(solution)/shard_map/ppermute | solution.py:641
  (21 other events, 301.8 us)
Sparse Core Ops, SparseCore 0:
  60.2 17.2 all-gather.2
